TPU v7x, 512 devices: a whole 4x8x8 slice. The times are simulated.
512 devices in a mesh: row: 64 (over z_hi, y, core), col: 8 (over z_lo, x).
Axes of the slice: x: 4, y: 8, z: 8 (z_hi: 4, z_lo: 2; z = z_hi * 2 + z_lo), core: 2. Of those that a mesh axis runs over, the one named last changes fastest.
Arguments:
- left: bfloat16 [1024, 49152], P('col', 'row'), may hold values from -0.02734375 to 0.02734375
- right: bfloat16 [49152, 4096], P('row', 'col'), may hold values from -6 to 6
- occupancy: int32 [16, 768], P('col', 'row'), may hold values from 0 to 1
- owners: int32 [8], replicated, may hold values from 0 to 7
- slab: bfloat16 [8, 128, 4096], P(None, 'row', 'col'), may hold values from -6 to 6
Outputs:
- updated: float32 [8, 128, 4096], P(None, 'row', 'col')
All inputs are finite; a program needn't handle non-finite values.
Results may differ from a plain program's by a relative error of at most 0.0005.
Values may be sent and summed in bfloat16 or wider, within the bound.
No kernel may reach another device: no remote copies, remote signals or barrier semaphores. Data moves between devices by JAX's collectives and lax.ppermute only.
A program may use at most 64 MiB of HBM per device.

v0:
```python
import jax
import jax.numpy as jnp
from jax import lax
from jax.sharding import PartitionSpec as P

ATOM_BLOCK = 64
STEPS = 8


def spread(block, axis, source):
    block = jnp.where(lax.axis_index(axis) == source, block, jnp.zeros_like(block))
    return lax.psum(block, axis)


def spread_marks(marks):
    values = marks.astype(jnp.bfloat16)
    count_r, count_c = values.shape
    return jnp.broadcast_to(
        values[:, None, :, None], (count_r, ATOM_BLOCK, count_c, ATOM_BLOCK)
    ).reshape(count_r * ATOM_BLOCK, count_c * ATOM_BLOCK)


def body(left, right, occupancy, owners, slab):
    panels = []
    for step in range(STEPS):
        owner = owners[step]
        piece, marks = (spread(left, "col", owner), spread(occupancy, "col", owner))
        panels.append(piece * spread_marks(marks))
    results = []
    for step in range(STEPS):
        kept = panels[step]
        summed = lax.psum_scatter(
            jnp.dot(kept, right, preferred_element_type=jnp.float32),
            "row",
            scatter_dimension=0,
            tiled=True,
        )
        results.append(1.5 * slab[step].astype(jnp.float32) - 0.5 * summed)
    return jnp.stack(results)


def solution(mesh):
    in_specs = (P("col", "row"), P("row", "col"), P("col", "row"), P(), P(None, "row", "col"))
    out_specs = P(None, "row", "col")
    return jax.shard_map(body, mesh=mesh, in_specs=in_specs, out_specs=out_specs, check_vma=False)
```

profile of v0, /device:TPU:1, one launch (start us, length us, event | category | flops | bytes accessed | tf_op | source)
XLA Modules:
  0.0 698.5 jit_solution(1302321162848097883)
XLA Ops:
  6.5 0.0 copy-start
  6.5 0.0 all-reduce.16.cloned.1.call-start
  6.5 0.7 copy-done.8
  7.3 0.7 fusion.32
  13.0 1.1 copy.22
  14.1 1.2 broadcast_select_fusion
  15.3 0.0 all-reduce.16.cloned.1.call-update
  15.3 0.0 all-reduce.14.cloned.1.call-start
  15.3 0.6 copy-done.10
  16.0 10.9 %all-reduce.8 = (s32[2,12]{1,0:T(2,128)S(1)}, s32[2,12]{1,0:T(2,128)S(1)}, s32[2,12]{1,0:T(2,128)S(1)}, s32[2,12]{1,0:T(2,128)S(1)}, s32[2,12]{1,0:T(2,128)S(1)}...) all-reduce(s32[2,12]{1,0:T(2,128)S(1)} %get-tuple-element.43, ...), channel_id=1, replica_groups=mesh['row'=64,'col'=8] {'col'}, use_global_device_ids=true, to_apply=%region_1.2 | all-reduce | flops 192 | bytes 1536 | tf_op jit(solution)/shard_map/psum | solution.py:12
  26.9 0.1 copy.37
  27.0 0.3 broadcast_in_dim.23
  27.3 0.2 reshape.63
  27.5 0.1 copy.27
  27.6 0.3 broadcast_in_dim.18
  27.9 0.2 reshape.58
  28.1 0.1 copy.25
  28.2 0.3 broadcast_in_dim.17
  28.5 0.2 reshape.57
  28.7 0.1 copy.35
  28.8 0.3 broadcast_in_dim.22
  29.1 0.2 reshape.62
  29.3 0.1 copy.33
  29.4 0.3 broadcast_in_dim.21
  29.7 0.2 reshape.61
  29.9 0.1 copy.31
  30.0 0.3 broadcast_in_dim.20
  30.3 0.2 reshape.60
  30.5 0.1 copy.29
  30.6 0.3 broadcast_in_dim.19
  30.9 0.2 reshape.59
  31.1 0.1 copy.23
  31.2 0.3 broadcast_in_dim.16
  31.5 0.2 reshape.56
  31.7 76.3 %all-reduce.16.cloned.1.call-done = (bf16[128,768]{0,1:T(8,128)(2,1)}, bf16[128,768]{0,1:T(8,128)(2,1)}, bf16[128,768]{0,1:T(8,128)(2,1)}, bf16[128,768]{0,1:T(8...) async-done(((bf16[128,768]{0,1:T(8,128)(2,1)}, bf16[128,768]{0,1:T(8,128)(2,1)}, ...) | async-done | bytes 1572880 | tf_op jit(solution)/shard_map/psum | solution.py:12
  108.0 0.0 copy-done
  108.0 1.9 fusion
  110.0 0.0 copy-done.7
  110.0 1.0 fusion.10
  111.0 0.0 copy-done.6
  111.0 1.0 fusion.12
  112.0 0.0 copy-done.5
  112.0 1.0 fusion.2
  113.0 0.0 copy-done.4
  113.0 1.0 fusion.4
  114.0 0.0 copy-done.3
  114.0 1.0 fusion.6
  115.0 0.0 copy-done.2
  115.0 1.0 fusion.8
  116.0 0.0 copy-done.1
  116.0 1.0 fusion.14
  117.0 0.0 all-reduce.14.cloned.1.call-update
  117.0 0.0 copy-start.9
  117.1 1.3 dynamic-slice
  119.0 565.7 %all-reduce.14.cloned.1.call-done = (f32[128,512]{1,0:T(8,128)}, f32[128,512]{1,0:T(8,128)}, f32[128,512]{1,0:T(8,128)}, f32[128,512]{1,0:T(8,128)}, f32[128,512...) async-done(((f32[128,512]{1,0:T(8,128)}, f32[128,512]{1,0:T(8,128)}, f32[128,512]{1,0:T(8,128)}, f32[128,512]{1,0:T(8,128)}, ...) | async-done | bytes 2097168
  684.6 0.7 constant_dynamic-update-slice_fusion.7
  685.4 0.7 constant_dynamic-update-slice_fusion.6
  686.1 0.7 constant_dynamic-update-slice_fusion.5
  686.8 0.7 constant_dynamic-update-slice_fusion.4
  687.6 0.7 constant_dynamic-update-slice_fusion.3
  688.3 0.7 constant_dynamic-update-slice_fusion.2
  689.0 0.7 constant_dynamic-update-slice_fusion.1
  689.8 0.6 copy-done.11
  690.4 1.3 constant_dynamic-update-slice_fusion
  (20 shorter events, 0.1 us)
Async XLA Ops:
  6.5 101.5 %copy-start = (bf16[768,512]{1,0:T(8,128)(2,1)S(1)}, bf16[768,512]{1,0:T(8,128)(2,1)}, u32[]{:S(2)}) copy-start(bf16[768,512]{1,0:T(8,128)(2,1)} %param.6) | copy-start | bytes 2359300
  6.5 0.7 copy-start.8
  6.5 101.5 %all-reduce.16.cloned.1.call-start = ((), (), s32[]{:S(2)}) async-start(), calls=%async_computation.1 | async-start | bytes 3145728 | tf_op jit(solution)/shard_map/psum | solution.py:12
  15.3 0.7 copy-start.10
  15.3 669.3 %all-reduce.14.cloned.1.call-start = ((), (), s32[]{:S(2)}) async-start(), calls=%async_computation | async-start | bytes 4194304
  108.0 2.0 copy-start.7
  110.0 1.0 copy-start.6
  111.0 1.0 copy-start.5
  112.0 1.0 copy-start.4
  113.0 1.0 copy-start.3
  114.0 1.0 copy-start.2
  115.0 1.0 copy-start.1
  117.0 567.6 %copy-start.9 = (bf16[8,2,512]{2,1,0:T(2,128)(2,1)S(1)}, bf16[8,2,512]{2,1,0:T(2,128)(2,1)}, u32[]{:S(2)}) copy-start(bf16[8,2,512]{2,1,0:T(2,128)(2,1)} %param.9) | copy-start | bytes 49156
  689.8 0.6 copy-start.11
Sparse Core Ops, SparseCore 0:
  15.4 92.5 all-reduce.15
  117.2 567.4 all-reduce.13
where the time goes:
time: 700 us; the launch traced here: 699 us
  waiting for transfers between devices  642 us (92%)
  between operations  19.3 us (3%)
  blocking collectives  10.9 us (2%)
  local copies, waits for them, and re-layouts  9.64 us (1%)
  matrix products  8.95 us (1%)
  other arithmetic  7.67 us (1%)
    unnamed x3, waiting for transfers between devices  566 us
    psum x1, waiting for transfers between devices, spread(): return lax.psum(block, axis)  76.3 us
  transfers between devices with their start and end apart: 2, of which 2 were waited for; matrix products, arithmetic and copies ran while one was open for 1% of the time, Pallas kernels for 0%

commit v1 on v0

v1 whole, which is shorter than its diff:
```python
import jax
import jax.numpy as jnp
from jax import lax
from jax.sharding import Mesh, PartitionSpec as P

ATOM_BLOCK = 64
STEPS = 8
PANEL_ROWS = 128
WIRE = jnp.float16
WIRE_SCALE_Y = 128.0
WIRE_SCALE_Z = 16.0


def shift(value, axis, count, by):
    return lax.ppermute(value, axis, [(i, (i + by) % count) for i in range(count)])


def row_order(y, zhi, core):
    place = lax.broadcasted_iota(jnp.int32, (64, PANEL_ROWS), 0)
    row = lax.broadcasted_iota(jnp.int32, (64, PANEL_ROWS), 1)
    s, u, b = place // 8, (place // 2) % 4, place % 2
    wanted = ((zhi + u) % 4) * 32 + ((y + s) % 8) * 4 + core * 2 + b
    return (row == wanted).astype(jnp.bfloat16)


def spread_marks(marks):
    values = marks.astype(jnp.bfloat16)
    count_r, count_c = values.shape
    return jnp.broadcast_to(
        values[:, None, :, None], (count_r, ATOM_BLOCK, count_c, ATOM_BLOCK)
    ).reshape(count_r * ATOM_BLOCK, count_c * ATOM_BLOCK)


def body(left, right, occupancy, owners, slab):
    zhi, y, core = (lax.axis_index(a) for a in ("zhi", "y", "core"))
    zlo, x = lax.axis_index("zlo"), lax.axis_index("x")

    depth, width = right.shape

    kept = left * spread_marks(occupancy)

    def pick(which):
        return jnp.dot(row_order(y, zhi, which), kept, preferred_element_type=jnp.float32).astype(jnp.bfloat16)

    right2 = shift(right, "core", 2, 1)
    mine = jnp.concatenate([pick(core), shift(pick(1 - core), "core", 2, 1)], axis=1)

    def ring(panel):
        from_left = shift(panel, "x", 4, 1)
        from_right = shift(panel, "x", 4, -1)
        far = jnp.concatenate(
            [shift(from_left[:32], "x", 4, 1), shift(from_right[32:], "x", 4, -1)], axis=0
        )
        return [panel, from_right, far, from_left]

    panels = ring(mine) + ring(shift(mine, "zlo", 2, 1))

    products = []
    for panel in panels:
        products.append(
            jnp.dot(panel[:, :depth], right, preferred_element_type=jnp.float32)
            + jnp.dot(panel[:, depth:], right2, preferred_element_type=jnp.float32)
        )
    product = jnp.stack(products).reshape(8, 8, 8, width)

    total = product[:, 0]
    for s in range(1, 8):
        got = shift((product[:, s] * WIRE_SCALE_Y).astype(WIRE), "y", 8, s)
        total = total + got.astype(jnp.float32) * (1.0 / WIRE_SCALE_Y)

    parts = total.reshape(8, 4, 2, width)
    summed = parts[:, 0]
    for u in range(1, 4):
        got = shift((parts[:, u] * WIRE_SCALE_Z).astype(WIRE), "zhi", 4, u)
        summed = summed + got.astype(jnp.float32) * (1.0 / WIRE_SCALE_Z)

    place = ((owners // 4) ^ zlo) * 4 + (owners % 4 - x) % 4
    chosen = place[:, None] == jnp.arange(8)[None, :]
    picked = jnp.sum(jnp.where(chosen[:, :, None, None], summed[None], 0.0), axis=1)
    return 1.5 * slab.astype(jnp.float32) - 0.5 * picked


def solution(mesh):
    fine = Mesh(mesh.devices.reshape(4, 8, 2, 2, 4), ("zhi", "y", "core", "zlo", "x"))
    row, col = ("zhi", "y", "core"), ("zlo", "x")
    in_specs = (P(col, row), P(row, col), P(col, row), P(), P(None, row, col))
    out_specs = P(None, row, col)
    return jax.shard_map(body, mesh=fine, in_specs=in_specs, out_specs=out_specs, check_vma=False)
```

time: 700 us -> 107 us (0.15)
  the two profiles are of different devices: /device:TPU:1 before, /device:TPU:6 now
where the time goes in v1:
time: 107 us; the launch traced here: 106 us
  starting transfers between devices  79 us (74%)
  waiting for transfers between devices  18.5 us (17%)
  matrix products  4.63 us (4%)
  local copies, waits for them, and re-layouts  2.38 us (2%)
  other arithmetic  1.16 us (1%)
    ppermute x21, starting transfers between devices, shift(): lax.ppermute(value, axis, [(i, (i + by) % count) for i in range(count)])  79 us
    ppermute x21, waiting for transfers between devices, shift(): lax.ppermute(value, axis, [(i, (i + by) % count) for i in range(count)])  18.5 us
  transfers between devices with their start and end apart: 21, of which 9 were waited for; matrix products, arithmetic and copies ran while one was open for 1% of the time, Pallas kernels for 0%

profile of v1, /device:TPU:6, one launch (start us, length us, event | category | flops | bytes accessed | tf_op | source)
XLA Modules:
  0.0 106.2 jit_solution(15998403389200832396)
XLA Ops:
  0.1 0.0 copy-start.3
  0.1 1.1 %copy.33 = bf16[128,768]{0,1:T(8,128)(2,1)S(1)} copy(bf16[128,768]{1,0:T(8,128)(2,1)} %param.5) | data formatting | bytes 393216 | tf_op args[0]
  1.2 0.1 copy.32
  1.3 0.3 broadcast_in_dim.31
  1.6 0.2 reshape.76
  1.8 0.3 convolution_convert_fusion
  2.1 0.0 copy-start
  2.1 2.1 %collective-permute-start = (bf16[64,768]{1,0:T(8,128)(2,1)S(1)}, bf16[64,768]{1,0:T(8,128)(2,1)S(1)}, u32[]{:S(2)}, u32[]{:S(2)}) collective-permute-start(bf16[64,768]{1,0:T(8,128)(2,1)S(1)} %convolution_convert_fusion), channel_id=1, source_target_pairs={{0,8},{8,0},{1,9},{9,1},{2,10},{10,2},{3,11},{11,3},{4,12},{12,4},... | collective-permute-start | bytes 294920 | tf_op jit(solution)/shard_map/ppermute | solution.py:15
  4.1 0.3 convolution_convert_fusion.1
  4.4 1.0 collective-permute-done
  5.4 7.7 %collective-permute-start.3 = (bf16[64,1536]{1,0:T(8,128)(2,1)S(1)}, bf16[64,1536]{1,0:T(8,128)(2,1)S(1)}, u32[]{:S(2)}, u32[]{:S(2)}) collective-permute-start(bf16[64,1536]{1,0:T(8,128)(2,1)S(1)} %pad_maximum_fusion), channel_id=1, source_target_pairs={{0,1},{1,2},{2,3},{3,0},{4,5},{5,6},{6,7},{7,4},{8,9},{9,10},{10,1... | collective-permute-start | bytes 589832 | tf_op jit(solution)/shard_map/ppermute | solution.py:15
  13.2 1.9 %collective-permute-start.1 = (bf16[768,512]{1,0:T(8,128)(2,1)S(1)}, bf16[768,512]{1,0:T(8,128)(2,1)S(1)}, u32[]{:S(2)}, u32[]{:S(2)}) collective-permute-start(bf16[768,512]{1,0:T(8,128)(2,1)S(1)} %copy-done), channel_id=1, source_target_pairs={{0,8},{8,0},{1,9},{9,1},{2,10},{10,2},{3,11},{11,3},{4,12},{12,4},... | collective-permute-start | bytes 2359304 | tf_op jit(solution)/shard_map/ppermute | solution.py:15
  15.1 1.9 %collective-permute-start.2 = (bf16[64,1536]{1,0:T(8,128)(2,1)S(1)}, bf16[64,1536]{1,0:T(8,128)(2,1)S(1)}, u32[]{:S(2)}, u32[]{:S(2)}) collective-permute-start(bf16[64,1536]{1,0:T(8,128)(2,1)S(1)} %pad_maximum_fusion), channel_id=1, source_target_pairs={{0,3},{1,0},{2,1},{3,2},{4,7},{5,4},{6,5},{7,6},{8,11},{9,8},{10,9... | collective-permute-start | bytes 589832 | tf_op jit(solution)/shard_map/ppermute | solution.py:15
  17.0 1.9 %collective-permute-start.6 = (bf16[64,1536]{1,0:T(8,128)(2,1)S(1)}, bf16[64,1536]{1,0:T(8,128)(2,1)S(1)}, u32[]{:S(2)}, u32[]{:S(2)}) collective-permute-start(bf16[64,1536]{1,0:T(8,128)(2,1)S(1)} %pad_maximum_fusion), channel_id=1, source_target_pairs={{0,4},{4,0},{1,5},{5,1},{2,6},{6,2},{3,7},{7,3},{8,12},{12,8},{9,1... | collective-permute-start | bytes 589832 | tf_op jit(solution)/shard_map/ppermute | solution.py:15
  19.0 5.1 %collective-permute-start.4 = (bf16[32,1536]{1,0:T(8,128)(2,1)S(1)}, bf16[32,1536]{1,0:T(8,128)(2,1)S(1)}, u32[]{:S(2)}, u32[]{:S(2)}) collective-permute-start(bf16[32,1536]{1,0:T(8,128)(2,1)S(1)} %slice.122), channel_id=1, source_target_pairs={{0,1},{1,2},{2,3},{3,0},{4,5},{5,6},{6,7},{7,4},{8,9},{9,10},{10,1... | collective-permute-start | bytes 294920 | tf_op jit(solution)/shard_map/ppermute | solution.py:15
  24.1 0.2 fusion.111
  24.4 1.1 %collective-permute-done.2 = bf16[64,1536]{1,0:T(8,128)(2,1)S(1)} collective-permute-done((bf16[64,1536]{1,0:T(8,128)(2,1)S(1)}, bf16[64,1536]{1,0:T(8,128)(2,1)S(1)}, u32[]{:S(2)}, u32[]{:S(2)}) %collective-permute-start.2) | collective-permute-done | bytes 196640 | tf_op jit(solution)/shard_map/ppermute | solution.py:15
  25.5 1.9 %collective-permute-start.5 = (bf16[32,1536]{1,0:T(8,128)(2,1)S(1)}, bf16[32,1536]{1,0:T(8,128)(2,1)S(1)}, u32[]{:S(2)}, u32[]{:S(2)}) collective-permute-start(bf16[32,1536]{1,0:T(8,128)(2,1)S(1)} %slice.123), channel_id=1, source_target_pairs={{0,3},{1,0},{2,1},{3,2},{4,7},{5,4},{6,5},{7,6},{8,11},{9,8},{10,9... | collective-permute-start | bytes 294920 | tf_op jit(solution)/shard_map/ppermute | solution.py:15
  27.5 1.9 %collective-permute-start.7 = (bf16[64,1536]{1,0:T(8,128)(2,1)S(1)}, bf16[64,1536]{1,0:T(8,128)(2,1)S(1)}, u32[]{:S(2)}, u32[]{:S(2)}) collective-permute-start(bf16[64,1536]{1,0:T(8,128)(2,1)S(1)} %collective-permute-done.6), channel_id=1, source_target_pairs={{0,3},{1,0},{2,1},{3,2},{4,7},{5,4},{6,5},{7,6},{8,11},{9,8},{10,9... | collective-permute-start | bytes 589832 | tf_op jit(solution)/shard_map/ppermute | solution.py:15
  29.4 5.1 %collective-permute-start.8 = (bf16[64,1536]{1,0:T(8,128)(2,1)S(1)}, bf16[64,1536]{1,0:T(8,128)(2,1)S(1)}, u32[]{:S(2)}, u32[]{:S(2)}) collective-permute-start(bf16[64,1536]{1,0:T(8,128)(2,1)S(1)} %collective-permute-done.6), channel_id=1, source_target_pairs={{0,1},{1,2},{2,3},{3,0},{4,5},{5,6},{6,7},{7,4},{8,9},{9,10},{10,1... | collective-permute-start | bytes 589832 | tf_op jit(solution)/shard_map/ppermute | solution.py:15
  34.6 3.7 %collective-permute-done.8 = bf16[64,1536]{1,0:T(8,128)(2,1)S(1)} collective-permute-done((bf16[64,1536]{1,0:T(8,128)(2,1)S(1)}, bf16[64,1536]{1,0:T(8,128)(2,1)S(1)}, u32[]{:S(2)}, u32[]{:S(2)}) %collective-permute-start.8) | collective-permute-done | bytes 196640 | tf_op jit(solution)/shard_map/ppermute | solution.py:15
  38.3 5.6 %collective-permute-start.9 = (bf16[32,1536]{1,0:T(8,128)(2,1)S(1)}, bf16[32,1536]{1,0:T(8,128)(2,1)S(1)}, u32[]{:S(2)}, u32[]{:S(2)}) collective-permute-start(bf16[32,1536]{1,0:T(8,128)(2,1)S(1)} %slice.132), channel_id=1, source_target_pairs={{0,1},{1,2},{2,3},{3,0},{4,5},{5,6},{6,7},{7,4},{8,9},{9,10},{10,1... | collective-permute-start | bytes 294920 | tf_op jit(solution)/shard_map/ppermute | solution.py:15
  44.0 1.9 %collective-permute-start.10 = (bf16[32,1536]{1,0:T(8,128)(2,1)S(1)}, bf16[32,1536]{1,0:T(8,128)(2,1)S(1)}, u32[]{:S(2)}, u32[]{:S(2)}) collective-permute-start(bf16[32,1536]{1,0:T(8,128)(2,1)S(1)} %slice.133), channel_id=1, source_target_pairs={{0,3},{1,0},{2,1},{3,2},{4,7},{5,4},{6,5},{7,6},{8,11},{9,8},{10,9... | collective-permute-start | bytes 294920 | tf_op jit(solution)/shard_map/ppermute | solution.py:15
  45.9 0.2 collective-permute-done.9
  46.1 5.6 %collective-permute-done.10 = bf16[32,1536]{1,0:T(8,128)(2,1)S(1)} collective-permute-done((bf16[32,1536]{1,0:T(8,128)(2,1)S(1)}, bf16[32,1536]{1,0:T(8,128)(2,1)S(1)}, u32[]{:S(2)}, u32[]{:S(2)}) %collective-permute-start.10) | collective-permute-done | bytes 98336 | tf_op jit(solution)/shard_map/ppermute | solution.py:15
  51.7 0.2 fusion.54
  51.9 0.3 fusion.15
  52.2 0.2 fusion.51
  52.5 0.3 fusion.13
  52.7 0.3 fusion.11
  53.0 0.2 fusion.48
  53.3 0.3 fusion.45
  53.5 0.3 fusion.42
  53.8 0.3 fusion.39
  54.0 0.3 fusion.9
  54.3 0.3 fusion.7
  54.6 0.3 fusion.5
  54.8 0.3 fusion.3
  55.1 0.2 fusion.36
  55.3 0.3 fusion.1
  55.6 1.9 %collective-permute-start.17 = (f16[8,8,512]{2,1,0:T(8,128)(2,1)S(1)}, f16[8,8,512]{2,1,0:T(8,128)(2,1)S(1)}, u32[]{:S(2)}, u32[]{:S(2)}) collective-permute-start(f16[8,8,512]{2,1,0:T(8,128)(2,1)S(1)} %fusion.65), channel_id=1, source_target_pairs={{0,112},{16,0},{32,16},{48,32},{64,48},{80,64},{96,80},{112,96},{1... | collective-permute-start | bytes 196616 | tf_op jit(solution)/shard_map/ppermute | solution.py:15
  57.6 0.1 fusion.59
  57.6 3.4 %collective-permute-start.16 = (f16[8,8,512]{2,1,0:T(8,128)(2,1)S(1)}, f16[8,8,512]{2,1,0:T(8,128)(2,1)S(1)}, u32[]{:S(2)}, u32[]{:S(2)}) collective-permute-start(f16[8,8,512]{2,1,0:T(8,128)(2,1)S(1)} %get-tuple-element.10), channel_id=1, source_target_pairs={{0,96},{16,112},{32,0},{48,16},{64,32},{80,48},{96,64},{112,80},{1... | collective-permute-start | bytes 196616 | tf_op jit(solution)/shard_map/ppermute | solution.py:15
  61.0 3.0 %collective-permute-start.15 = (f16[8,8,512]{2,1,0:T(8,128)(2,1)S(1)}, f16[8,8,512]{2,1,0:T(8,128)(2,1)S(1)}, u32[]{:S(2)}, u32[]{:S(2)}) collective-permute-start(f16[8,8,512]{2,1,0:T(8,128)(2,1)S(1)} %get-tuple-element.6), channel_id=1, source_target_pairs={{0,80},{16,96},{32,112},{48,0},{64,16},{80,32},{96,48},{112,64},{1... | collective-permute-start | bytes 196616 | tf_op jit(solution)/shard_map/ppermute | solution.py:15
  64.1 5.9 %collective-permute-start.14 = (f16[8,8,512]{2,1,0:T(8,128)(2,1)S(1)}, f16[8,8,512]{2,1,0:T(8,128)(2,1)S(1)}, u32[]{:S(2)}, u32[]{:S(2)}) collective-permute-start(f16[8,8,512]{2,1,0:T(8,128)(2,1)S(1)} %get-tuple-element.7), channel_id=1, source_target_pairs={{0,64},{16,80},{32,96},{48,112},{64,0},{80,16},{96,32},{112,48},{1... | collective-permute-start | bytes 196616 | tf_op jit(solution)/shard_map/ppermute | solution.py:15
  70.0 1.9 %collective-permute-start.13 = (f16[8,8,512]{2,1,0:T(8,128)(2,1)S(1)}, f16[8,8,512]{2,1,0:T(8,128)(2,1)S(1)}, u32[]{:S(2)}, u32[]{:S(2)}) collective-permute-start(f16[8,8,512]{2,1,0:T(8,128)(2,1)S(1)} %get-tuple-element.8), channel_id=1, source_target_pairs={{0,48},{16,64},{32,80},{48,96},{64,112},{80,0},{96,16},{112,32},{1... | collective-permute-start | bytes 196616 | tf_op jit(solution)/shard_map/ppermute | solution.py:15
  71.9 0.0 copy-start.2
  71.9 5.4 %collective-permute-start.12 = (f16[8,8,512]{2,1,0:T(8,128)(2,1)S(1)}, f16[8,8,512]{2,1,0:T(8,128)(2,1)S(1)}, u32[]{:S(2)}, u32[]{:S(2)}) collective-permute-start(f16[8,8,512]{2,1,0:T(8,128)(2,1)S(1)} %get-tuple-element.9), channel_id=1, source_target_pairs={{0,32},{16,48},{32,64},{48,80},{64,96},{80,112},{96,0},{112,16},{1... | collective-permute-start | bytes 196616 | tf_op jit(solution)/shard_map/ppermute | solution.py:15
  77.3 3.5 %collective-permute-start.11 = (f16[8,8,512]{2,1,0:T(8,128)(2,1)S(1)}, f16[8,8,512]{2,1,0:T(8,128)(2,1)S(1)}, u32[]{:S(2)}, u32[]{:S(2)}) collective-permute-start(f16[8,8,512]{2,1,0:T(8,128)(2,1)S(1)} %get-tuple-element.5), channel_id=1, source_target_pairs={{0,16},{16,32},{32,48},{48,64},{64,80},{80,96},{96,112},{112,0},{1... | collective-permute-start | bytes 196616 | tf_op jit(solution)/shard_map/ppermute | solution.py:15
  80.9 0.9 collective-permute-done.13
  81.8 0.6 collective-permute-done.12
  82.5 2.2 %collective-permute-done.11 = f16[8,8,512]{2,1,0:T(8,128)(2,1)S(1)} collective-permute-done((f16[8,8,512]{2,1,0:T(8,128)(2,1)S(1)}, f16[8,8,512]{2,1,0:T(8,128)(2,1)S(1)}, u32[]{:S(2)}, u32[]{:S(2)}) %collective-permute-start.11) | collective-permute-done | bytes 65568 | tf_op jit(solution)/shard_map/ppermute | solution.py:15
  84.7 0.1 fusion.35
  84.8 0.1 copy.46
  84.9 10.0 %collective-permute-start.20 = (f16[8,2,512]{2,0,1:T(8,128)(2,1)S(1)}, f16[8,2,512]{2,0,1:T(8,128)(2,1)S(1)}, u32[]{:S(2)}, u32[]{:S(2)}) collective-permute-start(f16[8,2,512]{2,0,1:T(8,128)(2,1)S(1)} %get-tuple-element.12), channel_id=1, source_target_pairs={{0,384},{128,0},{256,128},{384,256},{1,385},{129,1},{257,129},{385... | collective-permute-start | bytes 49160 | tf_op jit(solution)/shard_map/ppermute | solution.py:15
  95.0 1.9 %collective-permute-start.19 = (f16[8,2,512]{2,0,1:T(8,128)(2,1)S(1)}, f16[8,2,512]{2,0,1:T(8,128)(2,1)S(1)}, u32[]{:S(2)}, u32[]{:S(2)}) collective-permute-start(f16[8,2,512]{2,0,1:T(8,128)(2,1)S(1)} %get-tuple-element.13), channel_id=1, source_target_pairs={{0,256},{128,384},{256,0},{384,128},{1,257},{129,385},{257,1},{385... | collective-permute-start | bytes 49160 | tf_op jit(solution)/shard_map/ppermute | solution.py:15
  96.9 4.8 %collective-permute-start.18 = (f16[8,2,512]{2,0,1:T(8,128)(2,1)S(1)}, f16[8,2,512]{2,0,1:T(8,128)(2,1)S(1)}, u32[]{:S(2)}, u32[]{:S(2)}) collective-permute-start(f16[8,2,512]{2,0,1:T(8,128)(2,1)S(1)} %get-tuple-element.11), channel_id=1, source_target_pairs={{0,128},{128,256},{256,384},{384,0},{1,129},{129,257},{257,385},{3... | collective-permute-start | bytes 49160 | tf_op jit(solution)/shard_map/ppermute | solution.py:15
  101.7 0.1 iota_compare_fusion
  101.8 3.0 %collective-permute-done.19 = f16[8,2,512]{2,0,1:T(8,128)(2,1)S(1)} collective-permute-done((f16[8,2,512]{2,0,1:T(8,128)(2,1)S(1)}, f16[8,2,512]{2,0,1:T(8,128)(2,1)S(1)}, u32[]{:S(2)}, u32[]{:S(2)}) %collective-permute-start.19) | collective-permute-done | bytes 16416 | tf_op jit(solution)/shard_map/ppermute | solution.py:15
  104.8 0.0 collective-permute-done.18
  104.8 0.0 copy-start.1
  104.8 0.2 select_reduce_fusion
  105.0 0.5 copy-done.1
  105.5 0.6 multiply_subtract_fusion
  (33 shorter events, 0.2 us)
Async XLA Ops:
  0.1 1.1 %copy-start.3 = (s32[2,12]{1,0:T(2,128)S(1)}, s32[2,12]{1,0:T(2,128)}, u32[]{:S(2)}) copy-start(s32[2,12]{1,0:T(2,128)} %param.7) | copy-start | bytes 292
  2.1 11.1 %copy-start = (bf16[768,512]{1,0:T(8,128)(2,1)S(1)}, bf16[768,512]{1,0:T(8,128)(2,1)}, u32[]{:S(2)}) copy-start(bf16[768,512]{1,0:T(8,128)(2,1)} %param.6) | copy-start | bytes 2359300
  2.1 3.3 %collective-permute-start = (bf16[64,768]{1,0:T(8,128)(2,1)S(1)}, bf16[64,768]{1,0:T(8,128)(2,1)S(1)}, u32[]{:S(2)}, u32[]{:S(2)}) collective-permute-start(bf16[64,768]{1,0:T(8,128)(2,1)S(1)} %convolution_convert_fusion), channel_id=1, source_target_pairs={{0,8},{8,0},{1,9},{9,1},{2,10},{10,2},{3,11},{11,3},{4,12},{12,4},... | collective-permute-start | bytes 294920 | tf_op jit(solution)/shard_map/ppermute | solution.py:15
  5.4 13.6 %collective-permute-start.3 = (bf16[64,1536]{1,0:T(8,128)(2,1)S(1)}, bf16[64,1536]{1,0:T(8,128)(2,1)S(1)}, u32[]{:S(2)}, u32[]{:S(2)}) collective-permute-start(bf16[64,1536]{1,0:T(8,128)(2,1)S(1)} %pad_maximum_fusion), channel_id=1, source_target_pairs={{0,1},{1,2},{2,3},{3,0},{4,5},{5,6},{6,7},{7,4},{8,9},{9,10},{10,1... | collective-permute-start | bytes 589832 | tf_op jit(solution)/shard_map/ppermute | solution.py:15
  13.2 38.5 %collective-permute-start.1 = (bf16[768,512]{1,0:T(8,128)(2,1)S(1)}, bf16[768,512]{1,0:T(8,128)(2,1)S(1)}, u32[]{:S(2)}, u32[]{:S(2)}) collective-permute-start(bf16[768,512]{1,0:T(8,128)(2,1)S(1)} %copy-done), channel_id=1, source_target_pairs={{0,8},{8,0},{1,9},{9,1},{2,10},{10,2},{3,11},{11,3},{4,12},{12,4},... | collective-permute-start | bytes 2359304 | tf_op jit(solution)/shard_map/ppermute | solution.py:15
  15.1 10.4 %collective-permute-start.2 = (bf16[64,1536]{1,0:T(8,128)(2,1)S(1)}, bf16[64,1536]{1,0:T(8,128)(2,1)S(1)}, u32[]{:S(2)}, u32[]{:S(2)}) collective-permute-start(bf16[64,1536]{1,0:T(8,128)(2,1)S(1)} %pad_maximum_fusion), channel_id=1, source_target_pairs={{0,3},{1,0},{2,1},{3,2},{4,7},{5,4},{6,5},{7,6},{8,11},{9,8},{10,9... | collective-permute-start | bytes 589832 | tf_op jit(solution)/shard_map/ppermute | solution.py:15
  17.0 10.4 %collective-permute-start.6 = (bf16[64,1536]{1,0:T(8,128)(2,1)S(1)}, bf16[64,1536]{1,0:T(8,128)(2,1)S(1)}, u32[]{:S(2)}, u32[]{:S(2)}) collective-permute-start(bf16[64,1536]{1,0:T(8,128)(2,1)S(1)} %pad_maximum_fusion), channel_id=1, source_target_pairs={{0,4},{4,0},{1,5},{5,1},{2,6},{6,2},{3,7},{7,3},{8,12},{12,8},{9,1... | collective-permute-start | bytes 589832 | tf_op jit(solution)/shard_map/ppermute | solution.py:15
  19.0 15.5 %collective-permute-start.4 = (bf16[32,1536]{1,0:T(8,128)(2,1)S(1)}, bf16[32,1536]{1,0:T(8,128)(2,1)S(1)}, u32[]{:S(2)}, u32[]{:S(2)}) collective-permute-start(bf16[32,1536]{1,0:T(8,128)(2,1)S(1)} %slice.122), channel_id=1, source_target_pairs={{0,1},{1,2},{2,3},{3,0},{4,5},{5,6},{6,7},{7,4},{8,9},{9,10},{10,1... | collective-permute-start | bytes 294920 | tf_op jit(solution)/shard_map/ppermute | solution.py:15
  25.5 18.4 %collective-permute-start.5 = (bf16[32,1536]{1,0:T(8,128)(2,1)S(1)}, bf16[32,1536]{1,0:T(8,128)(2,1)S(1)}, u32[]{:S(2)}, u32[]{:S(2)}) collective-permute-start(bf16[32,1536]{1,0:T(8,128)(2,1)S(1)} %slice.123), channel_id=1, source_target_pairs={{0,3},{1,0},{2,1},{3,2},{4,7},{5,4},{6,5},{7,6},{8,11},{9,8},{10,9... | collective-permute-start | bytes 294920 | tf_op jit(solution)/shard_map/ppermute | solution.py:15
  27.5 16.5 %collective-permute-start.7 = (bf16[64,1536]{1,0:T(8,128)(2,1)S(1)}, bf16[64,1536]{1,0:T(8,128)(2,1)S(1)}, u32[]{:S(2)}, u32[]{:S(2)}) collective-permute-start(bf16[64,1536]{1,0:T(8,128)(2,1)S(1)} %collective-permute-done.6), channel_id=1, source_target_pairs={{0,3},{1,0},{2,1},{3,2},{4,7},{5,4},{6,5},{7,6},{8,11},{9,8},{10,9... | collective-permute-start | bytes 589832 | tf_op jit(solution)/shard_map/ppermute | solution.py:15
  29.4 8.9 %collective-permute-start.8 = (bf16[64,1536]{1,0:T(8,128)(2,1)S(1)}, bf16[64,1536]{1,0:T(8,128)(2,1)S(1)}, u32[]{:S(2)}, u32[]{:S(2)}) collective-permute-start(bf16[64,1536]{1,0:T(8,128)(2,1)S(1)} %collective-permute-done.6), channel_id=1, source_target_pairs={{0,1},{1,2},{2,3},{3,0},{4,5},{5,6},{6,7},{7,4},{8,9},{9,10},{10,1... | collective-permute-start | bytes 589832 | tf_op jit(solution)/shard_map/ppermute | solution.py:15
  38.3 7.8 %collective-permute-start.9 = (bf16[32,1536]{1,0:T(8,128)(2,1)S(1)}, bf16[32,1536]{1,0:T(8,128)(2,1)S(1)}, u32[]{:S(2)}, u32[]{:S(2)}) collective-permute-start(bf16[32,1536]{1,0:T(8,128)(2,1)S(1)} %slice.132), channel_id=1, source_target_pairs={{0,1},{1,2},{2,3},{3,0},{4,5},{5,6},{6,7},{7,4},{8,9},{9,10},{10,1... | collective-permute-start | bytes 294920 | tf_op jit(solution)/shard_map/ppermute | solution.py:15
  44.0 7.7 %collective-permute-start.10 = (bf16[32,1536]{1,0:T(8,128)(2,1)S(1)}, bf16[32,1536]{1,0:T(8,128)(2,1)S(1)}, u32[]{:S(2)}, u32[]{:S(2)}) collective-permute-start(bf16[32,1536]{1,0:T(8,128)(2,1)S(1)} %slice.133), channel_id=1, source_target_pairs={{0,3},{1,0},{2,1},{3,2},{4,7},{5,4},{6,5},{7,6},{8,11},{9,8},{10,9... | collective-permute-start | bytes 294920 | tf_op jit(solution)/shard_map/ppermute | solution.py:15
  55.6 16.3 %collective-permute-start.17 = (f16[8,8,512]{2,1,0:T(8,128)(2,1)S(1)}, f16[8,8,512]{2,1,0:T(8,128)(2,1)S(1)}, u32[]{:S(2)}, u32[]{:S(2)}) collective-permute-start(f16[8,8,512]{2,1,0:T(8,128)(2,1)S(1)} %fusion.65), channel_id=1, source_target_pairs={{0,112},{16,0},{32,16},{48,32},{64,48},{80,64},{96,80},{112,96},{1... | collective-permute-start | bytes 196616 | tf_op jit(solution)/shard_map/ppermute | solution.py:15
  57.6 19.7 %collective-permute-start.16 = (f16[8,8,512]{2,1,0:T(8,128)(2,1)S(1)}, f16[8,8,512]{2,1,0:T(8,128)(2,1)S(1)}, u32[]{:S(2)}, u32[]{:S(2)}) collective-permute-start(f16[8,8,512]{2,1,0:T(8,128)(2,1)S(1)} %get-tuple-element.10), channel_id=1, source_target_pairs={{0,96},{16,112},{32,0},{48,16},{64,32},{80,48},{96,64},{112,80},{1... | collective-permute-start | bytes 196616 | tf_op jit(solution)/shard_map/ppermute | solution.py:15
  61.0 19.9 %collective-permute-start.15 = (f16[8,8,512]{2,1,0:T(8,128)(2,1)S(1)}, f16[8,8,512]{2,1,0:T(8,128)(2,1)S(1)}, u32[]{:S(2)}, u32[]{:S(2)}) collective-permute-start(f16[8,8,512]{2,1,0:T(8,128)(2,1)S(1)} %get-tuple-element.6), channel_id=1, source_target_pairs={{0,80},{16,96},{32,112},{48,0},{64,16},{80,32},{96,48},{112,64},{1... | collective-permute-start | bytes 196616 | tf_op jit(solution)/shard_map/ppermute | solution.py:15
  64.1 16.8 %collective-permute-start.14 = (f16[8,8,512]{2,1,0:T(8,128)(2,1)S(1)}, f16[8,8,512]{2,1,0:T(8,128)(2,1)S(1)}, u32[]{:S(2)}, u32[]{:S(2)}) collective-permute-start(f16[8,8,512]{2,1,0:T(8,128)(2,1)S(1)} %get-tuple-element.7), channel_id=1, source_target_pairs={{0,64},{16,80},{32,96},{48,112},{64,0},{80,16},{96,32},{112,48},{1... | collective-permute-start | bytes 196616 | tf_op jit(solution)/shard_map/ppermute | solution.py:15
  70.0 11.8 %collective-permute-start.13 = (f16[8,8,512]{2,1,0:T(8,128)(2,1)S(1)}, f16[8,8,512]{2,1,0:T(8,128)(2,1)S(1)}, u32[]{:S(2)}, u32[]{:S(2)}) collective-permute-start(f16[8,8,512]{2,1,0:T(8,128)(2,1)S(1)} %get-tuple-element.8), channel_id=1, source_target_pairs={{0,48},{16,64},{32,80},{48,96},{64,112},{80,0},{96,16},{112,32},{1... | collective-permute-start | bytes 196616 | tf_op jit(solution)/shard_map/ppermute | solution.py:15
  71.9 8.9 %copy-start.2 = (s32[8]{0:T(128)S(1)}, s32[8]{0:T(128)}, u32[]{:S(2)}) copy-start(s32[8]{0:T(128)} %param.8) | copy-start | bytes 100
  71.9 10.5 %collective-permute-start.12 = (f16[8,8,512]{2,1,0:T(8,128)(2,1)S(1)}, f16[8,8,512]{2,1,0:T(8,128)(2,1)S(1)}, u32[]{:S(2)}, u32[]{:S(2)}) collective-permute-start(f16[8,8,512]{2,1,0:T(8,128)(2,1)S(1)} %get-tuple-element.9), channel_id=1, source_target_pairs={{0,32},{16,48},{32,64},{48,80},{64,96},{80,112},{96,0},{112,16},{1... | collective-permute-start | bytes 196616 | tf_op jit(solution)/shard_map/ppermute | solution.py:15
  77.3 7.4 %collective-permute-start.11 = (f16[8,8,512]{2,1,0:T(8,128)(2,1)S(1)}, f16[8,8,512]{2,1,0:T(8,128)(2,1)S(1)}, u32[]{:S(2)}, u32[]{:S(2)}) collective-permute-start(f16[8,8,512]{2,1,0:T(8,128)(2,1)S(1)} %get-tuple-element.5), channel_id=1, source_target_pairs={{0,16},{16,32},{32,48},{48,64},{64,80},{80,96},{96,112},{112,0},{1... | collective-permute-start | bytes 196616 | tf_op jit(solution)/shard_map/ppermute | solution.py:15
  84.9 16.9 %collective-permute-start.20 = (f16[8,2,512]{2,0,1:T(8,128)(2,1)S(1)}, f16[8,2,512]{2,0,1:T(8,128)(2,1)S(1)}, u32[]{:S(2)}, u32[]{:S(2)}) collective-permute-start(f16[8,2,512]{2,0,1:T(8,128)(2,1)S(1)} %get-tuple-element.12), channel_id=1, source_target_pairs={{0,384},{128,0},{256,128},{384,256},{1,385},{129,1},{257,129},{385... | collective-permute-start | bytes 49160 | tf_op jit(solution)/shard_map/ppermute | solution.py:15
  95.0 9.8 %collective-permute-start.19 = (f16[8,2,512]{2,0,1:T(8,128)(2,1)S(1)}, f16[8,2,512]{2,0,1:T(8,128)(2,1)S(1)}, u32[]{:S(2)}, u32[]{:S(2)}) collective-permute-start(f16[8,2,512]{2,0,1:T(8,128)(2,1)S(1)} %get-tuple-element.13), channel_id=1, source_target_pairs={{0,256},{128,384},{256,0},{384,128},{1,257},{129,385},{257,1},{385... | collective-permute-start | bytes 49160 | tf_op jit(solution)/shard_map/ppermute | solution.py:15
  96.9 7.9 %collective-permute-start.18 = (f16[8,2,512]{2,0,1:T(8,128)(2,1)S(1)}, f16[8,2,512]{2,0,1:T(8,128)(2,1)S(1)}, u32[]{:S(2)}, u32[]{:S(2)}) collective-permute-start(f16[8,2,512]{2,0,1:T(8,128)(2,1)S(1)} %get-tuple-element.11), channel_id=1, source_target_pairs={{0,128},{128,256},{256,384},{384,0},{1,129},{129,257},{257,385},{3... | collective-permute-start | bytes 49160 | tf_op jit(solution)/shard_map/ppermute | solution.py:15
  104.8 0.7 copy-start.1

commit v2 on v0

v2 whole, which is shorter than its diff:
```python
import jax
import jax.numpy as jnp
from jax import lax
from jax.sharding import Mesh, PartitionSpec as P

ATOM_BLOCK = 64
PANEL_ROWS = 128
WIRE_SCALE = 2.0**18


def row_order():
    place = lax.broadcasted_iota(jnp.int32, (PANEL_ROWS, PANEL_ROWS), 0)
    row = lax.broadcasted_iota(jnp.int32, (PANEL_ROWS, PANEL_ROWS), 1)
    core, at, b = place // 64, (place % 64) // 2, place % 2
    return (row == at * 4 + core * 2 + b).astype(jnp.bfloat16)


def spread_marks(marks):
    values = marks.astype(jnp.bfloat16)
    count_r, count_c = values.shape
    return jnp.broadcast_to(
        values[:, None, :, None], (count_r, ATOM_BLOCK, count_c, ATOM_BLOCK)
    ).reshape(count_r * ATOM_BLOCK, count_c * ATOM_BLOCK)


def body(left, right, occupancy, owners, slab):
    core = lax.axis_index("core")
    depth, width = right.shape

    right2 = lax.ppermute(right, "core", [(0, 1), (1, 0)])

    kept = left * spread_marks(occupancy)
    halves = jnp.dot(row_order(), kept, preferred_element_type=jnp.float32).astype(jnp.bfloat16)
    sent = jnp.broadcast_to(halves.reshape(2, 1, 64, depth), (2, 8, 64, depth)).reshape(16, 64, depth)
    panels = lax.all_to_all(sent, ("core", "zlo", "x"), 0, 0, tiled=True).reshape(2, 512, depth)

    own = lax.dynamic_index_in_dim(panels, core, 0, keepdims=False)
    other = lax.dynamic_index_in_dim(panels, 1 - core, 0, keepdims=False)
    product = jnp.dot(own, right, preferred_element_type=jnp.float32) + jnp.dot(
        other, right2, preferred_element_type=jnp.float32
    )

    parts = jnp.round(product * WIRE_SCALE).astype(jnp.int32).reshape(8, 32, 2, width).transpose(1, 0, 2, 3).reshape(32, 16, width)
    total = lax.psum_scatter(parts, ("zhi", "y"), scatter_dimension=0, tiled=True)
    summed = total.astype(jnp.float32).reshape(8, 2, width) * (1.0 / WIRE_SCALE)

    chosen = owners[:, None] == jnp.arange(8)[None, :]
    picked = jnp.sum(jnp.where(chosen[:, :, None, None], summed[None], 0.0), axis=1)
    return 1.5 * slab.astype(jnp.float32) - 0.5 * picked


def solution(mesh):
    fine = Mesh(mesh.devices.reshape(4, 8, 2, 2, 4), ("zhi", "y", "core", "zlo", "x"))
    row, col = ("zhi", "y", "core"), ("zlo", "x")
    in_specs = (P(col, row), P(row, col), P(col, row), P(), P(None, row, col))
    out_specs = P(None, row, col)
    return jax.shard_map(body, mesh=fine, in_specs=in_specs, out_specs=out_specs, check_vma=False)
```

time: 700 us -> 374 us (0.53)
  the two profiles are of different devices: /device:TPU:1 before, /device:TPU:4 now
where the time goes in v2:
time: 374 us
  waiting for transfers between devices  337 us (90%)
  between operations  13.5 us (4%)
  starting transfers between devices  11.6 us (3%)
  local copies, waits for them, and re-layouts  6.75 us (2%)
    unnamed x2, waiting for transfers between devices  319 us
    all_to_all x1, waiting for transfers between devices, body(): lax.all_to_all(sent, ('core', 'zlo', 'x'), 0, 0, tiled=True)  18 us
    all_to_all x1, starting transfers between devices, body(): lax.all_to_all(sent, ('core', 'zlo', 'x'), 0, 0, tiled=True)  9.51 us
  transfers between devices with their start and end apart: 3, of which 2 were waited for; matrix products, arithmetic and copies ran while one was open for 1% of the time, Pallas kernels for 0%

profile of v2, /device:TPU:4, one launch (start us, length us, event | category | flops | bytes accessed | tf_op | source)
XLA Modules:
  0.0 373.9 jit_solution(15722989238639809072)
XLA Ops:
  6.6 0.7 convert_element_type.17
  7.3 0.1 copy.13
  7.4 0.3 broadcast_in_dim.38
  7.6 0.2 reshape.47
  7.9 1.1 copy.14
  8.9 0.4 convolution_convert_fusion
  9.3 1.3 broadcast_in_dim.40
  10.6 0.0 copy-start
  10.6 9.5 %all-to-all-start = ((bf16[16,64,768]{2,1,0:T(8,128)(2,1)}), bf16[16,64,768]{2,1,0:T(8,128)(2,1)S(1)}, u32[]{:S(2)}, u32[]{:S(2)}) async-start(bf16[16,64,768]{2,1,0:T(8,128)(2,1)} %bitcast.1), calls=%async_computation | async-start | bytes 3145728 | tf_op jit(solution)/shard_map/all_to_all | solution.py:35
  20.1 0.0 all-reduce.3.cloned.1.call-start
  20.2 0.0 copy-done
  20.2 2.1 collective-permute-start
  22.3 18.0 %all-to-all-done = bf16[16,64,768]{2,1,0:T(8,128)(2,1)S(1)} async-done(((bf16[16,64,768]{2,1,0:T(8,128)(2,1)}), bf16[16,64,768]{2,1,0:T(8,128)(2,1)S(1)}, u32[]{:S(2)}, u32[]{:S(2)}) %all-to-all-start) | async-done | bytes 1572896 | tf_op jit(solution)/shard_map/all_to_all | solution.py:35
  40.3 0.6 fusion.4
  40.8 0.0 collective-permute-done
  40.9 0.6 fusion.2
  41.4 0.6 reshape.50
  42.1 0.2 copy.15
  42.3 0.0 copy-start.2
  42.3 0.0 copy-start.1
  42.3 1.6 copy.16
  43.9 0.0 all-reduce.3.cloned.1.call-update
  44.0 1.3 dynamic-slice
  45.2 0.0 copy-done.2
  45.2 0.1 iota_compare_fusion
  45.3 319.4 %all-reduce.3.cloned.1.call-done = s32[32,16,512]{2,1,0:T(8,128)} async-done(((s32[32,16,512]{2,1,0:T(8,128)}), s32[32,16,512]{2,1,0:T(8,128)}) %all-reduce.3.cloned.1.call-update) | async-done | bytes 1048592
  364.8 1.4 fusion.21
  366.2 0.2 select_reduce_fusion
  366.4 0.0 copy-done.1
  366.4 0.6 multiply_subtract_fusion
  (7 shorter events, 0.1 us)
Async XLA Ops:
  10.6 9.6 %copy-start = (bf16[768,512]{1,0:T(8,128)(2,1)S(1)}, bf16[768,512]{1,0:T(8,128)(2,1)}, u32[]{:S(2)}) copy-start(bf16[768,512]{1,0:T(8,128)(2,1)} %param.6) | copy-start | bytes 2359300
  10.6 29.7 %all-to-all-start = ((bf16[16,64,768]{2,1,0:T(8,128)(2,1)}), bf16[16,64,768]{2,1,0:T(8,128)(2,1)S(1)}, u32[]{:S(2)}, u32[]{:S(2)}) async-start(bf16[16,64,768]{2,1,0:T(8,128)(2,1)} %bitcast.1), calls=%async_computation | async-start | bytes 3145728 | tf_op jit(solution)/shard_map/all_to_all | solution.py:35
  20.1 344.6 %all-reduce.3.cloned.1.call-start = ((), (), s32[]{:S(2)}) async-start(), calls=%async_computation.1 | async-start | bytes 2097152
  20.2 20.7 %collective-permute-start = (bf16[768,512]{1,0:T(8,128)(2,1)S(1)}, bf16[768,512]{1,0:T(8,128)(2,1)S(1)}, u32[]{:S(2)}, u32[]{:S(2)}) collective-permute-start(bf16[768,512]{1,0:T(8,128)(2,1)S(1)} %copy-done), channel_id=1, source_target_pairs={{0,8},{8,0},{1,9},{9,1},{2,10},{10,2},{3,11},{11,3},{4,12},{12,4},... | collective-permute-start | bytes 2359304 | tf_op jit(solution)/shard_map/ppermute | solution.py:30
  42.3 3.0 copy-start.2
  42.3 324.1 %copy-start.1 = (bf16[8,2,512]{2,1,0:T(2,128)(2,1)S(1)}, bf16[8,2,512]{2,1,0:T(2,128)(2,1)}, u32[]{:S(2)}) copy-start(bf16[8,2,512]{2,1,0:T(2,128)(2,1)} %param.9) | copy-start | bytes 49156
Sparse Core Ops, SparseCore 0:
  44.1 320.6 all-reduce.2

commit v3 on v2

v3 whole, which is shorter than its diff:
```python
import jax
import jax.numpy as jnp
from jax import lax
from jax.experimental import pallas as pl
from jax.experimental.pallas import tpu as pltpu
from jax.sharding import Mesh, PartitionSpec as P

ATOM_BLOCK = 64
PANEL_ROWS = 128
HALF = 64
SLOTS = 8
LANES = 128
PACKED_ROWS = SLOTS // 2 * 32
LIST_ROWS = 16
WIRE = jnp.float16
WIRE_SCALE = 128.0


def row_order():
    place = lax.broadcasted_iota(jnp.int32, (PANEL_ROWS, PANEL_ROWS), 0)
    row = lax.broadcasted_iota(jnp.int32, (PANEL_ROWS, PANEL_ROWS), 1)
    core, at, b = place // HALF, (place % HALF) // 2, place % 2
    return (row == at * 4 + core * 2 + b).astype(jnp.bfloat16)


def pack_kernel(marks_ref, left_ref, out_ref, rows, tiles):
    rows[...] = jnp.dot(row_order(), left_ref[...], preferred_element_type=jnp.float32).astype(jnp.bfloat16)
    tiles[...] = jnp.zeros_like(tiles)
    lane = lax.broadcasted_iota(jnp.int32, (32, LANES), 1)
    list_lane = lax.broadcasted_iota(jnp.int32, (LIST_ROWS, LANES), 1)
    block_rows, block_cols = marks_ref.shape
    count = jnp.int32(0)
    listed = jnp.zeros((LIST_ROWS, LANES), jnp.float32)
    for i in range(block_rows):
        for j in range(block_cols):
            kept = marks_ref[i, j] != 0
            slot = jnp.minimum(count, SLOTS - 1)
            fits = jnp.logical_and(kept, count < SLOTS)

            @pl.when(fits)
            def _(i=i, j=j, slot=slot):
                side = lax.rem(slot, 2)
                here = lane // ATOM_BLOCK == side
                at = pl.ds(pl.multiple_of(lax.div(slot, 2) * 32, 32), 32)
                for half in range(2):
                    block = rows[half * HALF + i * 32 : half * HALF + i * 32 + 32, j // 2 * LANES : (j // 2 + 1) * LANES]
                    turned = pltpu.roll(block, ATOM_BLOCK, 1)
                    placed = jnp.where(side == j % 2, block, turned)
                    tiles[half, at, :] = jnp.where(here, placed, tiles[half, at, :])

            mark = jnp.where(fits, 1.0, 0.0)
            listed = listed + jnp.where(list_lane == slot, mark * i, 0.0)
            listed = listed + jnp.where(list_lane == slot + 16, mark * j, 0.0)
            count = count + kept.astype(jnp.int32)
    listed = listed + jnp.where(list_lane == 32, count.astype(jnp.float32), 0.0)
    for to in range(out_ref.shape[0]):
        out_ref[to, :PACKED_ROWS, :] = tiles[to // 8]
        out_ref[to, PACKED_ROWS:, :] = listed.astype(jnp.bfloat16)


def product_kernel(core_ref, got_ref, right_ref, right2_ref, out_ref, dense, lists, places, sem):
    sources = got_ref.shape[0]
    depth = right_ref.shape[0]
    core = core_ref[0]
    for source in range(sources):
        lists[source * 8 : source * 8 + 8, :] = got_ref[source, PACKED_ROWS:, :].astype(jnp.int32)[:8]
    copy = pltpu.make_async_copy(lists, places, sem)
    copy.start()
    dense[...] = jnp.zeros_like(dense)
    copy.wait()
    lane = lax.broadcasted_iota(jnp.int32, (32, LANES), 1)

    def one_source(source, too_many):
        count = places[source * 8, 32]
        first = jnp.where(source // 8 == core, 0, depth)
        top = lax.rem(source, 8) * HALF

        def one_block(slot, carry):
            i = places[source * 8, slot]
            j = places[source * 8, slot + 16]
            block = got_ref[source, pl.ds(pl.multiple_of(lax.div(slot, 2) * 32, 32), 32), :]
            side = lax.rem(j, 2)
            placed = jnp.where(side == lax.rem(slot, 2), block, pltpu.roll(block, ATOM_BLOCK, 1))
            to_rows = pl.ds(pl.multiple_of(top + i * 32, 32), 32)
            to_lanes = pl.ds(pl.multiple_of(first + lax.div(j, 2) * LANES, LANES), LANES)
            dense[to_rows, to_lanes] = jnp.where(lane // ATOM_BLOCK == side, placed, dense[to_rows, to_lanes])
            return carry

        lax.fori_loop(0, jnp.minimum(count, SLOTS), one_block, 0)
        return jnp.logical_or(too_many, count > SLOTS)

    too_many = lax.fori_loop(0, sources, one_source, jnp.bool_(False))
    for m in range(0, out_ref.shape[0], 128):
        out_ref[m : m + 128, :] = jnp.dot(
            dense[m : m + 128, :depth], right_ref[...], preferred_element_type=jnp.float32
        ) + jnp.dot(dense[m : m + 128, depth:], right2_ref[...], preferred_element_type=jnp.float32)

    @pl.when(too_many)
    def _():
        out_ref[...] = jnp.full(out_ref.shape, jnp.nan, jnp.float32)


def pack(marks, left):
    return pl.pallas_call(
        pack_kernel,
        out_shape=jax.ShapeDtypeStruct((16, PACKED_ROWS + LIST_ROWS, LANES), jnp.bfloat16),
        in_specs=[pl.BlockSpec(memory_space=pltpu.SMEM), pl.BlockSpec(memory_space=pltpu.VMEM)],
        out_specs=pl.BlockSpec(memory_space=pltpu.VMEM),
        scratch_shapes=[
            pltpu.VMEM(left.shape, jnp.bfloat16),
            pltpu.VMEM((2, PACKED_ROWS, LANES), jnp.bfloat16),
        ],
    )(marks, left)


def unpack_product(core, got, right, right2):
    depth, width = right.shape
    return pl.pallas_call(
        product_kernel,
        out_shape=jax.ShapeDtypeStruct((8 * HALF, width), jnp.float32),
        in_specs=[pl.BlockSpec(memory_space=pltpu.SMEM)] + [pl.BlockSpec(memory_space=pltpu.VMEM)] * 3,
        out_specs=pl.BlockSpec(memory_space=pltpu.VMEM),
        scratch_shapes=[
            pltpu.VMEM((8 * HALF, 2 * depth), jnp.bfloat16),
            pltpu.VMEM((16 * 8, LANES), jnp.int32),
            pltpu.SMEM((16 * 8, LANES), jnp.int32),
            pltpu.SemaphoreType.DMA,
        ],
        compiler_params=pltpu.CompilerParams(vmem_limit_bytes=24 * 2**20),
        cost_estimate=pl.CostEstimate(flops=2 * 8 * HALF * 2 * depth * width, bytes_accessed=4 * 2**20, transcendentals=0),
    )(core.reshape(1), got, right, right2)


def spread_marks(marks):
    values = marks.astype(jnp.bfloat16)
    count_r, count_c = values.shape
    return jnp.broadcast_to(
        values[:, None, :, None], (count_r, ATOM_BLOCK, count_c, ATOM_BLOCK)
    ).reshape(count_r * ATOM_BLOCK, count_c * ATOM_BLOCK)


def dense_product(core, left, right, right2, occupancy):
    depth = right.shape[0]
    kept = left * spread_marks(occupancy)
    halves = jnp.dot(row_order(), kept, preferred_element_type=jnp.float32).astype(jnp.bfloat16)
    sent = jnp.broadcast_to(halves.reshape(2, 1, HALF, depth), (2, 8, HALF, depth)).reshape(16, HALF, depth)
    panels = lax.all_to_all(sent, ("core", "zlo", "x"), 0, 0, tiled=True).reshape(2, 8 * HALF, depth)
    own = lax.dynamic_index_in_dim(panels, core, 0, keepdims=False)
    other = lax.dynamic_index_in_dim(panels, 1 - core, 0, keepdims=False)
    return jnp.dot(own, right, preferred_element_type=jnp.float32) + jnp.dot(
        other, right2, preferred_element_type=jnp.float32
    )


def reduce_rows(product):
    width = product.shape[-1]
    parts = (product * WIRE_SCALE).astype(WIRE).reshape(8, 32, 2, width).transpose(1, 0, 2, 3)
    got = lax.all_to_all(parts, ("zhi", "y"), 0, 0, tiled=True)
    return jnp.sum(got.astype(jnp.float32), axis=0) * (1.0 / WIRE_SCALE)


def body(left, right, occupancy, owners, slab):
    core = lax.axis_index("core")

    right2 = lax.ppermute(right, "core", [(0, 1), (1, 0)])

    got = lax.all_to_all(pack(occupancy, left), ("core", "zlo", "x"), 0, 0, tiled=True)
    summed = reduce_rows(unpack_product(core, got, right, right2))

    summed = lax.cond(
        jnp.isnan(summed[0, 0, 0]),
        lambda: reduce_rows(dense_product(core, left, right, right2, occupancy)),
        lambda: summed,
    )

    chosen = owners[:, None] == jnp.arange(8)[None, :]
    picked = jnp.sum(jnp.where(chosen[:, :, None, None], summed[None], 0.0), axis=1)
    return 1.5 * slab.astype(jnp.float32) - 0.5 * picked


def solution(mesh):
    fine = Mesh(mesh.devices.reshape(4, 8, 2, 2, 4), ("zhi", "y", "core", "zlo", "x"))
    row, col = ("zhi", "y", "core"), ("zlo", "x")
    in_specs = (P(col, row), P(row, col), P(col, row), P(), P(None, row, col))
    out_specs = P(None, row, col)
    return jax.shard_map(body, mesh=fine, in_specs=in_specs, out_specs=out_specs, check_vma=False)
```

time: 374 us -> 66.6 us (0.18)
  the two profiles are of different devices: /device:TPU:4 before, /device:TPU:8 now
where the time goes in v3:
time: 66.6 us; the launch traced here: 66.2 us
  waiting for transfers between devices  29.6 us (44%)
  starting transfers between devices  23.5 us (35%)
  Pallas kernels  7.53 us (11%)
  local copies, waits for them, and re-layouts  2.72 us (4%)
  other arithmetic  1.46 us (2%)
  between operations  1.4 us (2%)
    all_to_all x1, waiting for transfers between devices, reduce_rows(): got = lax.all_to_all(parts, ('zhi', 'y'), 0, 0, tiled=True)  20.6 us
    all_to_all x1, starting transfers between devices, reduce_rows(): got = lax.all_to_all(parts, ('zhi', 'y'), 0, 0, tiled=True)  15 us
    all_to_all x1, waiting for transfers between devices, body(): lax.all_to_all(pack(occupancy, left), ('core', 'zlo', 'x'), 0, 0, tiled=T...  7.15 us
    all_to_all x1, starting transfers between devices, body(): lax.all_to_all(pack(occupancy, left), ('core', 'zlo', 'x'), 0, 0, tiled=T...  6.14 us
    pallas_call x1, Pallas kernels, unpack_product(): pl.pallas_call(product_kernel, out_shape=jax.ShapeDtypeStruct((8 * HALF,...  5.03 us
    pallas_call x1, Pallas kernels, pack(): pl.pallas_call(pack_kernel, out_shape=jax.ShapeDtypeStruct((16, PACKED_RO...  2.5 us
    ppermute x1, starting transfers between devices, body(): right2 = lax.ppermute(right, 'core', [(0, 1), (1, 0)])  2.32 us
    ppermute x1, waiting for transfers between devices, body(): right2 = lax.ppermute(right, 'core', [(0, 1), (1, 0)])  1.89 us
  transfers between devices with their start and end apart: 3, of which 3 were waited for; matrix products, arithmetic and copies ran while one was open for 0% of the time, Pallas kernels for 0%

profile of v3, /device:TPU:8, one launch (start us, length us, event | category | flops | bytes accessed | tf_op | source)
XLA Modules:
  0.0 66.2 jit_solution(17128219121059259681)
XLA Ops:
  0.0 0.0 copy-start
  0.0 2.5 %shard_map.55 = bf16[16,144,128]{2,1,0:T(8,128)(2,1)} custom-call(s32[2,12]{1,0:T(2,128)} %marks_ref.1, bf16[128,768]{1,0:T(8,128)(2,1)} %left_ref.1), custom_call_target="tpu_custom_call" | custom-call | tf_op jit(solution)/shard_map/pallas_call | solution.py:104
  2.5 6.1 %all-to-all-start.2 = ((bf16[16,144,128]{2,1,0:T(8,128)(2,1)}), bf16[16,144,128]{2,1,0:T(8,128)(2,1)S(1)}, u32[]{:S(2)}, u32[]{:S(2)}) async-start(bf16[16,144,128]{2,1,0:T(8,128)(2,1)} %shard_map.55), calls=%async_computation.2 | async-start | bytes 1179648 | tf_op jit(solution)/shard_map/all_to_all | solution.py:167
  8.7 0.0 copy-done
  8.7 2.3 %collective-permute-start = (bf16[768,512]{1,0:T(8,128)(2,1)S(1)}, bf16[768,512]{1,0:T(8,128)(2,1)S(1)}, u32[]{:S(2)}, u32[]{:S(2)}) collective-permute-start(bf16[768,512]{1,0:T(8,128)(2,1)S(1)} %copy-done), channel_id=1, source_target_pairs={{0,8},{8,0},{1,9},{9,1},{2,10},{10,2},{3,11},{11,3},{4,12},{12,4},... | collective-permute-start | bytes 2359304 | tf_op jit(solution)/shard_map/ppermute | solution.py:165
  11.0 1.9 %collective-permute-done.right2_ref = bf16[768,512]{1,0:T(8,128)(2,1)S(1)} collective-permute-done((bf16[768,512]{1,0:T(8,128)(2,1)S(1)}, bf16[768,512]{1,0:T(8,128)(2,1)S(1)}, u32[]{:S(2)}, u32[]{:S(2)}) %collective-permute-start) | collective-permute-done | bytes 786464 | tf_op jit(solution)/shard_map/ppermute | solution.py:165
  12.9 7.1 %all-to-all-done.2.got_ref = bf16[16,144,128]{2,1,0:T(8,128)(2,1)S(1)} async-done(((bf16[16,144,128]{2,1,0:T(8,128)(2,1)}), bf16[16,144,128]{2,1,0:T(8,128)(2,1)S(1)}, u32[]{:S(2)}, u32[]{:S(2)}) %all-to-all-start.2) | async-done | bytes 589856 | tf_op jit(solution)/shard_map/all_to_all | solution.py:167
  20.0 5.0 %shard_map.56 = f32[512,512]{1,0:T(8,128)S(1)} custom-call(s32[1]{0:T(128)} %bitcast.6.core_ref, bf16[16,144,128]{2,1,0:T(8,128)(2,1)S(1)} %all-to-all-done.2.got_ref, bf16[768,512]{1,0:T(8,128)(2,1)S(1)} %copy-done, bf16[768,512]{1,0:T(8,128)(2,1)S(1)} %collective-permute-done.right2_ref), custom_call_target="tpu_custom_call" | custom-call | flops 805306368 | bytes 4194304 | tf_op jit(solution)/shard_map/pallas_call | solution.py:118
  25.1 0.1 multiply_convert_fusion
  25.2 0.0 copy-start.4
  25.2 0.3 reshape.47
  25.5 0.0 copy-start.1
  25.5 0.0 copy-start.3
  25.5 1.4 %copy.20 = f16[8,32,2,512]{3,2,0,1:T(2,128)(2,1)} copy(f16[8,32,2,512]{3,2,1,0:T(2,128)(2,1)S(1)} %reshape.47) | data formatting | bytes 1048576 | tf_op jit(solution)/shard_map/reshape | solution.py:157
  26.9 15.0 %all-to-all-start.3 = ((f16[32,8,2,512]{3,2,1,0:T(2,128)(2,1)}), f16[32,8,2,512]{3,2,1,0:T(2,128)(2,1)S(1)}, u32[]{:S(2)}, u32[]{:S(2)}) async-start(f16[32,8,2,512]{3,2,1,0:T(2,128)(2,1)} %bitcast.20), calls=%async_computation.3 | async-start | bytes 1048576 | tf_op jit(solution)/shard_map/all_to_all | solution.py:158
  41.9 0.0 copy-done.4
  41.9 0.1 iota_compare_fusion
  42.0 20.6 %all-to-all-done.3 = f16[32,8,2,512]{3,2,1,0:T(2,128)(2,1)S(1)} async-done(((f16[32,8,2,512]{3,2,1,0:T(2,128)(2,1)}), f16[32,8,2,512]{3,2,1,0:T(2,128)(2,1)S(1)}, u32[]{:S(2)}, u32[]{:S(2)}) %all-to-all-start.3) | async-done | bytes 524320 | tf_op jit(solution)/shard_map/all_to_all | solution.py:158
  62.6 0.4 convert_reduce_fusion.1
  63.0 0.6 slice.4
  64.8 0.0 copy-done.1
  64.8 0.0 copy-done.3
  64.9 0.0 copy-start.2
  64.9 0.2 select_reduce_fusion
  65.1 0.5 copy-done.2
  65.6 0.6 multiply_subtract_fusion
  (3 shorter events, 0.0 us)
Async XLA Ops:
  0.0 8.7 %copy-start = (bf16[768,512]{1,0:T(8,128)(2,1)S(1)}, bf16[768,512]{1,0:T(8,128)(2,1)}, u32[]{:S(2)}) copy-start(bf16[768,512]{1,0:T(8,128)(2,1)} %right_ref.1) | copy-start | bytes 2359300
  2.5 17.5 %all-to-all-start.2 = ((bf16[16,144,128]{2,1,0:T(8,128)(2,1)}), bf16[16,144,128]{2,1,0:T(8,128)(2,1)S(1)}, u32[]{:S(2)}, u32[]{:S(2)}) async-start(bf16[16,144,128]{2,1,0:T(8,128)(2,1)} %shard_map.55), calls=%async_computation.2 | async-start | bytes 1179648 | tf_op jit(solution)/shard_map/all_to_all | solution.py:167
  8.7 4.2 %collective-permute-start = (bf16[768,512]{1,0:T(8,128)(2,1)S(1)}, bf16[768,512]{1,0:T(8,128)(2,1)S(1)}, u32[]{:S(2)}, u32[]{:S(2)}) collective-permute-start(bf16[768,512]{1,0:T(8,128)(2,1)S(1)} %copy-done), channel_id=1, source_target_pairs={{0,8},{8,0},{1,9},{9,1},{2,10},{10,2},{3,11},{11,3},{4,12},{12,4},... | collective-permute-start | bytes 2359304 | tf_op jit(solution)/shard_map/ppermute | solution.py:165
  25.2 16.7 %copy-start.4 = (s32[8]{0:T(128)S(1)}, s32[8]{0:T(128)}, u32[]{:S(2)}) copy-start(s32[8]{0:T(128)} %param.10) | copy-start | bytes 100
  25.5 39.4 %copy-start.1 = (bf16[128,768]{1,0:T(8,128)(2,1)S(1)}, bf16[128,768]{1,0:T(8,128)(2,1)}, u32[]{:S(2)}) copy-start(bf16[128,768]{1,0:T(8,128)(2,1)} %left_ref.1) | copy-start | bytes 589828
  25.5 39.4 %copy-start.3 = (s32[2,12]{1,0:T(2,128)S(1)}, s32[2,12]{1,0:T(2,128)}, u32[]{:S(2)}) copy-start(s32[2,12]{1,0:T(2,128)} %marks_ref.1) | copy-start | bytes 292
  26.9 35.7 %all-to-all-start.3 = ((f16[32,8,2,512]{3,2,1,0:T(2,128)(2,1)}), f16[32,8,2,512]{3,2,1,0:T(2,128)(2,1)S(1)}, u32[]{:S(2)}, u32[]{:S(2)}) async-start(f16[32,8,2,512]{3,2,1,0:T(2,128)(2,1)} %bitcast.20), calls=%async_computation.3 | async-start | bytes 1048576 | tf_op jit(solution)/shard_map/all_to_all | solution.py:158
  64.9 0.7 %copy-start.2 = (bf16[8,2,512]{2,1,0:T(2,128)(2,1)S(1)}, bf16[8,2,512]{2,1,0:T(2,128)(2,1)}, u32[]{:S(2)}) copy-start(bf16[8,2,512]{2,1,0:T(2,128)(2,1)} %param.11) | copy-start | bytes 49156

commit v4 on v3

--- a/solution.py
+++ b/solution.py
@@ -14,6 +14,7 @@
 LIST_ROWS = 16
 WIRE = jnp.float16
 WIRE_SCALE = 128.0
+PAIR_SCALE = 64.0
 
 
 def row_order():
@@ -58,12 +59,20 @@
         out_ref[to, PACKED_ROWS:, :] = listed.astype(jnp.bfloat16)
 
 
-def product_kernel(core_ref, got_ref, right_ref, right2_ref, out_ref, dense, lists, places, sem):
+def destination_order(parity):
+    place = lax.broadcasted_iota(jnp.int32, (256, 256), 0)
+    row = lax.broadcasted_iota(jnp.int32, (256, 256), 1)
+    away, zhi, pair, panel, b = place // 128, place // 64 % 2, place // 16 % 4, place // 2 % 8, place % 2
+    y = 2 * pair + (parity + away) % 2
+    return (row == panel * 32 + zhi * 16 + y * 2 + b).astype(jnp.bfloat16)
+
+
+def product_kernel(at_ref, got_ref, right_ref, right2_ref, keep_ref, send_ref, dense, lists, places, sem):
     sources = got_ref.shape[0]
     depth = right_ref.shape[0]
-    core = core_ref[0]
+    core, parity = at_ref[0], at_ref[1]
     for source in range(sources):
-        lists[source * 8 : source * 8 + 8, :] = got_ref[source, PACKED_ROWS:, :].astype(jnp.int32)[:8]
+        lists[source : source + 1, :] = got_ref[source, PACKED_ROWS : PACKED_ROWS + 1, :].astype(jnp.int32)
     copy = pltpu.make_async_copy(lists, places, sem)
     copy.start()
     dense[...] = jnp.zeros_like(dense)
@@ -71,17 +80,17 @@
     lane = lax.broadcasted_iota(jnp.int32, (32, LANES), 1)
 
     def one_source(source, too_many):
-        count = places[source * 8, 32]
-        first = jnp.where(source // 8 == core, 0, depth)
-        top = lax.rem(source, 8) * HALF
+        count = places[source, 32]
+        first = jnp.where(lax.div(source, 8) == core, 0, depth)
+        panel = lax.rem(source, 8) * 32
 
         def one_block(slot, carry):
-            i = places[source * 8, slot]
-            j = places[source * 8, slot + 16]
+            i = places[source, slot]
+            j = places[source, slot + 16]
             block = got_ref[source, pl.ds(pl.multiple_of(lax.div(slot, 2) * 32, 32), 32), :]
             side = lax.rem(j, 2)
             placed = jnp.where(side == lax.rem(slot, 2), block, pltpu.roll(block, ATOM_BLOCK, 1))
-            to_rows = pl.ds(pl.multiple_of(top + i * 32, 32), 32)
+            to_rows = pl.ds(pl.multiple_of(i * 256 + panel, 32), 32)
             to_lanes = pl.ds(pl.multiple_of(first + lax.div(j, 2) * LANES, LANES), LANES)
             dense[to_rows, to_lanes] = jnp.where(lane // ATOM_BLOCK == side, placed, dense[to_rows, to_lanes])
             return carry
@@ -90,14 +99,19 @@
         return jnp.logical_or(too_many, count > SLOTS)
 
     too_many = lax.fori_loop(0, sources, one_source, jnp.bool_(False))
-    for m in range(0, out_ref.shape[0], 128):
-        out_ref[m : m + 128, :] = jnp.dot(
-            dense[m : m + 128, :depth], right_ref[...], preferred_element_type=jnp.float32
-        ) + jnp.dot(dense[m : m + 128, depth:], right2_ref[...], preferred_element_type=jnp.float32)
+    order = destination_order(parity)
+    for i in range(2):
+        rows = jnp.dot(order, dense[i * 256 : i * 256 + 256, :], preferred_element_type=jnp.float32).astype(jnp.bfloat16)
+        sums = jnp.dot(rows[:, :depth], right_ref[...], preferred_element_type=jnp.float32) + jnp.dot(
+            rows[:, depth:], right2_ref[...], preferred_element_type=jnp.float32
+        )
+        keep_ref[i * 128 : i * 128 + 128, :] = sums[:128]
+        send_ref[i * 128 : i * 128 + 128, :] = sums[128:]
 
     @pl.when(too_many)
     def _():
-        out_ref[...] = jnp.full(out_ref.shape, jnp.nan, jnp.float32)
+        keep_ref[...] = jnp.full(keep_ref.shape, jnp.nan, jnp.float32)
+        send_ref[...] = jnp.full(send_ref.shape, jnp.nan, jnp.float32)
 
 
 def pack(marks, left):
@@ -113,22 +127,22 @@
     )(marks, left)
 
 
-def unpack_product(core, got, right, right2):
+def unpack_product(core, parity, got, right, right2):
     depth, width = right.shape
     return pl.pallas_call(
         product_kernel,
-        out_shape=jax.ShapeDtypeStruct((8 * HALF, width), jnp.float32),
+        out_shape=[jax.ShapeDtypeStruct((256, width), jnp.float32)] * 2,
         in_specs=[pl.BlockSpec(memory_space=pltpu.SMEM)] + [pl.BlockSpec(memory_space=pltpu.VMEM)] * 3,
-        out_specs=pl.BlockSpec(memory_space=pltpu.VMEM),
+        out_specs=[pl.BlockSpec(memory_space=pltpu.VMEM)] * 2,
         scratch_shapes=[
-            pltpu.VMEM((8 * HALF, 2 * depth), jnp.bfloat16),
-            pltpu.VMEM((16 * 8, LANES), jnp.int32),
-            pltpu.SMEM((16 * 8, LANES), jnp.int32),
+            pltpu.VMEM((512, 2 * depth), jnp.bfloat16),
+            pltpu.VMEM((16, LANES), jnp.int32),
+            pltpu.SMEM((16, LANES), jnp.int32),
             pltpu.SemaphoreType.DMA,
         ],
         compiler_params=pltpu.CompilerParams(vmem_limit_bytes=24 * 2**20),
-        cost_estimate=pl.CostEstimate(flops=2 * 8 * HALF * 2 * depth * width, bytes_accessed=4 * 2**20, transcendentals=0),
-    )(core.reshape(1), got, right, right2)
+        cost_estimate=pl.CostEstimate(flops=2 * 512 * 2 * depth * width, bytes_accessed=4 * 2**20, transcendentals=0),
+    )(jnp.stack([core, parity]), got, right, right2)
 
 
 def spread_marks(marks):
@@ -152,24 +166,33 @@
     )
 
 
-def reduce_rows(product):
+def reduce_dense(product):
     width = product.shape[-1]
     parts = (product * WIRE_SCALE).astype(WIRE).reshape(8, 32, 2, width).transpose(1, 0, 2, 3)
-    got = lax.all_to_all(parts, ("zhi", "y"), 0, 0, tiled=True)
+    got = lax.all_to_all(parts, ("zhi", "pair", "parity"), 0, 0, tiled=True)
     return jnp.sum(got.astype(jnp.float32), axis=0) * (1.0 / WIRE_SCALE)
 
 
+def reduce_rows(keep, send):
+    width = keep.shape[-1]
+    came = lax.ppermute((send * WIRE_SCALE).astype(WIRE), "parity", [(0, 1), (1, 0)])
+    total = keep + came.astype(jnp.float32) * (1.0 / WIRE_SCALE)
+    parts = (total * PAIR_SCALE).astype(WIRE).reshape(16, 16, width)
+    got = lax.all_to_all(parts, ("zhi", "pair"), 0, 0, tiled=True)
+    return (jnp.sum(got.astype(jnp.float32), axis=0) * (1.0 / PAIR_SCALE)).reshape(8, 2, width)
+
+
 def body(left, right, occupancy, owners, slab):
-    core = lax.axis_index("core")
+    core, parity = lax.axis_index("core"), lax.axis_index("parity")
 
     right2 = lax.ppermute(right, "core", [(0, 1), (1, 0)])
 
     got = lax.all_to_all(pack(occupancy, left), ("core", "zlo", "x"), 0, 0, tiled=True)
-    summed = reduce_rows(unpack_product(core, got, right, right2))
+    summed = reduce_rows(*unpack_product(core, parity, got, right, right2))
 
     summed = lax.cond(
         jnp.isnan(summed[0, 0, 0]),
-        lambda: reduce_rows(dense_product(core, left, right, right2, occupancy)),
+        lambda: reduce_dense(dense_product(core, left, right, right2, occupancy)),
         lambda: summed,
     )
 
@@ -179,8 +202,8 @@
 
 
 def solution(mesh):
-    fine = Mesh(mesh.devices.reshape(4, 8, 2, 2, 4), ("zhi", "y", "core", "zlo", "x"))
-    row, col = ("zhi", "y", "core"), ("zlo", "x")
+    fine = Mesh(mesh.devices.reshape(4, 4, 2, 2, 2, 4), ("zhi", "pair", "parity", "core", "zlo", "x"))
+    row, col = ("zhi", "pair", "parity", "core"), ("zlo", "x")
     in_specs = (P(col, row), P(row, col), P(col, row), P(), P(None, row, col))
     out_specs = P(None, row, col)
     return jax.shard_map(body, mesh=fine, in_specs=in_specs, out_specs=out_specs, check_vma=False)

time: 66.6 us -> 68.9 us (1.035)
  the two profiles are of different devices: /device:TPU:8 before, /device:TPU:1 now
where the time goes in v4:
time: 68.9 us; the launch traced here: 68.2 us
  waiting for transfers between devices  29.9 us (43%)
  starting transfers between devices  25.8 us (37%)
  Pallas kernels  8.14 us (12%)
  other arithmetic  1.86 us (3%)
  between operations  1.44 us (2%)
  local copies, waits for them, and re-layouts  1.08 us (2%)
    all_to_all x1, waiting for transfers between devices, reduce_rows(): got = lax.all_to_all(parts, ('zhi', 'pair'), 0, 0, tiled=True)  13.1 us
    all_to_all x1, starting transfers between devices, reduce_rows(): got = lax.all_to_all(parts, ('zhi', 'pair'), 0, 0, tiled=True)  11.5 us
    all_to_all x1, starting transfers between devices, body(): lax.all_to_all(pack(occupancy, left), ('core', 'zlo', 'x'), 0, 0, tiled=T...  10.2 us
    ppermute x1, waiting for transfers between devices, reduce_rows(): lax.ppermute((send * WIRE_SCALE).astype(WIRE), 'parity', [(0, 1), (1, 0)])  7.64 us
    all_to_all x1, waiting for transfers between devices, body(): lax.all_to_all(pack(occupancy, left), ('core', 'zlo', 'x'), 0, 0, tiled=T...  7.08 us
    pallas_call x1, Pallas kernels, unpack_product(): pl.pallas_call(product_kernel, out_shape=[jax.ShapeDtypeStruct((256, widt...  5.64 us
    pallas_call x1, Pallas kernels, pack(): pl.pallas_call(pack_kernel, out_shape=jax.ShapeDtypeStruct((16, PACKED_RO...  2.5 us
    ppermute x1, starting transfers between devices, body(): right2 = lax.ppermute(right, 'core', [(0, 1), (1, 0)])  2.08 us
  transfers between devices with their start and end apart: 4, of which 4 were waited for; matrix products, arithmetic and copies ran while one was open for 0% of the time, Pallas kernels for 0%

profile of v4, /device:TPU:1, one launch (start us, length us, event | category | flops | bytes accessed | tf_op | source)
XLA Modules:
  0.0 68.2 jit_solution(11864140056829832774)
XLA Ops:
  0.0 0.0 copy-start.1
  0.0 2.5 %shard_map.55 = bf16[16,144,128]{2,1,0:T(8,128)(2,1)} custom-call(s32[2,12]{1,0:T(2,128)} %marks_ref.1, bf16[128,768]{1,0:T(8,128)(2,1)} %left_ref.1), custom_call_target="tpu_custom_call" | custom-call | tf_op jit(solution)/shard_map/pallas_call | solution.py:118
  2.5 10.2 %all-to-all-start.2 = ((bf16[16,144,128]{2,1,0:T(8,128)(2,1)}), bf16[16,144,128]{2,1,0:T(8,128)(2,1)S(1)}, u32[]{:S(2)}, u32[]{:S(2)}) async-start(bf16[16,144,128]{2,1,0:T(8,128)(2,1)} %shard_map.55), calls=%async_computation.2 | async-start | bytes 1179648 | tf_op jit(solution)/shard_map/all_to_all | solution.py:190
  12.7 0.0 copy-done.1
  12.7 2.1 %collective-permute-start = (bf16[768,512]{1,0:T(8,128)(2,1)S(1)}, bf16[768,512]{1,0:T(8,128)(2,1)S(1)}, u32[]{:S(2)}, u32[]{:S(2)}) collective-permute-start(bf16[768,512]{1,0:T(8,128)(2,1)S(1)} %copy-done.1), channel_id=1, source_target_pairs={{0,8},{8,0},{1,9},{9,1},{2,10},{10,2},{3,11},{11,3},{4,12},{12,4},... | collective-permute-start | bytes 2359304 | tf_op jit(solution)/shard_map/ppermute | solution.py:188
  14.8 0.1 pad_add_fusion.at_ref
  14.8 2.0 %collective-permute-done.right2_ref = bf16[768,512]{1,0:T(8,128)(2,1)S(1)} collective-permute-done((bf16[768,512]{1,0:T(8,128)(2,1)S(1)}, bf16[768,512]{1,0:T(8,128)(2,1)S(1)}, u32[]{:S(2)}, u32[]{:S(2)}) %collective-permute-start) | collective-permute-done | bytes 786464 | tf_op jit(solution)/shard_map/ppermute | solution.py:188
  16.9 7.1 %all-to-all-done.2.got_ref = bf16[16,144,128]{2,1,0:T(8,128)(2,1)S(1)} async-done(((bf16[16,144,128]{2,1,0:T(8,128)(2,1)}), bf16[16,144,128]{2,1,0:T(8,128)(2,1)S(1)}, u32[]{:S(2)}, u32[]{:S(2)}) %all-to-all-start.2) | async-done | bytes 589856 | tf_op jit(solution)/shard_map/all_to_all | solution.py:190
  23.9 5.6 %shard_map.56 = (f32[256,512]{1,0:T(8,128)S(1)}, f32[256,512]{1,0:T(8,128)S(1)}) custom-call(s32[2]{0:T(128)S(1)} %pad_add_fusion.at_ref, bf16[16,144,128]{2,1,0:T(8,128)(2,1)S(1)} %all-to-all-done.2.got_ref, bf16[768,512]{1,0:T(8,128)(2,1)S(1)} %copy-done.1, bf16[768,512]{1,0:T(8,128)(2,1)S(1)} %collective-permute-done.right2_ref), custom_call_target="tpu_custom_call" | custom-call | flops 805306368 | bytes 4194304 | tf_op jit(solution)/shard_map/pallas_call | solution.py:132
  29.6 0.0 copy-start.4
  29.6 0.0 copy-start
  29.6 0.0 copy-start.3
  29.7 2.1 %collective-permute-start.1 = (f16[256,512]{1,0:T(8,128)(2,1)S(1)}, f16[256,512]{1,0:T(8,128)(2,1)S(1)}, u32[]{:S(2)}, u32[]{:S(2)}) collective-permute-start(f16[256,512]{1,0:T(8,128)(2,1)S(1)} %multiply_convert_fusion.1), channel_id=1, source_target_pairs={{0,16},{16,0},{1,17},{17,1},{2,18},{18,2},{3,19},{19,3},{4,20},{20... | collective-permute-start | bytes 786440 | tf_op jit(solution)/shard_map/ppermute | solution.py:178
  31.7 7.6 %collective-permute-done.1 = f16[256,512]{1,0:T(8,128)(2,1)S(1)} collective-permute-done((f16[256,512]{1,0:T(8,128)(2,1)S(1)}, f16[256,512]{1,0:T(8,128)(2,1)S(1)}, u32[]{:S(2)}, u32[]{:S(2)}) %collective-permute-start.1) | collective-permute-done | bytes 262176 | tf_op jit(solution)/shard_map/ppermute | solution.py:178
  39.4 0.8 %multiply_convert_fusion = f16[256,512]{1,0:T(8,128)(2,1)} fusion(f32[256,512]{1,0:T(8,128)S(1)} %get-tuple-element.26, f16[256,512]{1,0:T(8,128)(2,1)S(1)} %collective-permute-done.1), kind=kLoop, calls=%fused_computation.61 | loop fusion | flops 655360 | bytes 1048576 | tf_op jit(solution)/shard_map/convert_element_type | solution.py:180
  40.2 11.5 %all-to-all-start.3 = ((f16[16,16,512]{2,1,0:T(8,128)(2,1)}), f16[16,16,512]{2,1,0:T(8,128)(2,1)S(1)}, u32[]{:S(2)}, u32[]{:S(2)}) async-start(f16[16,16,512]{2,1,0:T(8,128)(2,1)} %bitcast.8), calls=%async_computation.3 | async-start | bytes 524288 | tf_op jit(solution)/shard_map/all_to_all | solution.py:181
  51.7 0.0 copy-done.4
  51.7 0.1 iota_compare_fusion
  51.8 13.1 %all-to-all-done.3 = f16[16,16,512]{2,1,0:T(8,128)(2,1)S(1)} async-done(((f16[16,16,512]{2,1,0:T(8,128)(2,1)}), f16[16,16,512]{2,1,0:T(8,128)(2,1)S(1)}, u32[]{:S(2)}, u32[]{:S(2)}) %all-to-all-start.3) | async-done | bytes 262176 | tf_op jit(solution)/shard_map/all_to_all | solution.py:181
  65.0 0.5 slice.4
  66.8 0.0 copy-done
  66.8 0.0 copy-done.3
  66.8 0.0 copy-start.2
  66.9 0.2 select_reduce_fusion
  67.0 0.5 copy-done.2
  67.5 0.6 multiply_subtract_fusion
  (6 shorter events, 0.1 us)
Async XLA Ops:
  0.0 12.7 %copy-start.1 = (bf16[768,512]{1,0:T(8,128)(2,1)S(1)}, bf16[768,512]{1,0:T(8,128)(2,1)}, u32[]{:S(2)}) copy-start(bf16[768,512]{1,0:T(8,128)(2,1)} %right_ref.1) | copy-start | bytes 2359300
  2.5 21.4 %all-to-all-start.2 = ((bf16[16,144,128]{2,1,0:T(8,128)(2,1)}), bf16[16,144,128]{2,1,0:T(8,128)(2,1)S(1)}, u32[]{:S(2)}, u32[]{:S(2)}) async-start(bf16[16,144,128]{2,1,0:T(8,128)(2,1)} %shard_map.55), calls=%async_computation.2 | async-start | bytes 1179648 | tf_op jit(solution)/shard_map/all_to_all | solution.py:190
  12.7 4.2 %collective-permute-start = (bf16[768,512]{1,0:T(8,128)(2,1)S(1)}, bf16[768,512]{1,0:T(8,128)(2,1)S(1)}, u32[]{:S(2)}, u32[]{:S(2)}) collective-permute-start(bf16[768,512]{1,0:T(8,128)(2,1)S(1)} %copy-done.1), channel_id=1, source_target_pairs={{0,8},{8,0},{1,9},{9,1},{2,10},{10,2},{3,11},{11,3},{4,12},{12,4},... | collective-permute-start | bytes 2359304 | tf_op jit(solution)/shard_map/ppermute | solution.py:188
  29.6 22.1 %copy-start.4 = (s32[8]{0:T(128)S(1)}, s32[8]{0:T(128)}, u32[]{:S(2)}) copy-start(s32[8]{0:T(128)} %param.10) | copy-start | bytes 100
  29.6 37.2 %copy-start = (bf16[128,768]{1,0:T(8,128)(2,1)S(1)}, bf16[128,768]{1,0:T(8,128)(2,1)}, u32[]{:S(2)}) copy-start(bf16[128,768]{1,0:T(8,128)(2,1)} %left_ref.1) | copy-start | bytes 589828
  29.6 37.2 %copy-start.3 = (s32[2,12]{1,0:T(2,128)S(1)}, s32[2,12]{1,0:T(2,128)}, u32[]{:S(2)}) copy-start(s32[2,12]{1,0:T(2,128)} %marks_ref.1) | copy-start | bytes 292
  29.7 9.7 %collective-permute-start.1 = (f16[256,512]{1,0:T(8,128)(2,1)S(1)}, f16[256,512]{1,0:T(8,128)(2,1)S(1)}, u32[]{:S(2)}, u32[]{:S(2)}) collective-permute-start(f16[256,512]{1,0:T(8,128)(2,1)S(1)} %multiply_convert_fusion.1), channel_id=1, source_target_pairs={{0,16},{16,0},{1,17},{17,1},{2,18},{18,2},{3,19},{19,3},{4,20},{20... | collective-permute-start | bytes 786440 | tf_op jit(solution)/shard_map/ppermute | solution.py:178
  40.2 24.7 %all-to-all-start.3 = ((f16[16,16,512]{2,1,0:T(8,128)(2,1)}), f16[16,16,512]{2,1,0:T(8,128)(2,1)S(1)}, u32[]{:S(2)}, u32[]{:S(2)}) async-start(f16[16,16,512]{2,1,0:T(8,128)(2,1)} %bitcast.8), calls=%async_computation.3 | async-start | bytes 524288 | tf_op jit(solution)/shard_map/all_to_all | solution.py:181
  66.8 0.7 %copy-start.2 = (bf16[8,2,512]{2,1,0:T(2,128)(2,1)S(1)}, bf16[8,2,512]{2,1,0:T(2,128)(2,1)}, u32[]{:S(2)}) copy-start(bf16[8,2,512]{2,1,0:T(2,128)(2,1)} %param.11) | copy-start | bytes 49156

commit v5 on v3

--- a/solution.py
+++ b/solution.py
@@ -1,3 +1,5 @@
+import functools
+
 import jax
 import jax.numpy as jnp
 from jax import lax
@@ -10,6 +12,8 @@
 HALF = 64
 SLOTS = 8
 LANES = 128
+TILE = 8
+DISTINCT = (4, 5, 6, 8)
 PACKED_ROWS = SLOTS // 2 * 32
 LIST_ROWS = 16
 WIRE = jnp.float16
@@ -58,42 +62,66 @@
         out_ref[to, PACKED_ROWS:, :] = listed.astype(jnp.bfloat16)
 
 
-def product_kernel(core_ref, got_ref, right_ref, right2_ref, out_ref, dense, lists, places, sem):
+def destination_order(owners_ref, slots):
+    shape = (32 * slots, 256)
+    place = lax.broadcasted_iota(jnp.int32, shape, 0)
+    row = lax.broadcasted_iota(jnp.int32, shape, 1)
+    at, slot, b = place // (2 * slots), place // 2 % slots, place % 2
+    wanted = at * 2 + b
+    filled = jnp.int32(0)
+    for panel in range(8):
+        owned = functools.reduce(jnp.logical_or, [owners_ref[t] == panel for t in range(owners_ref.shape[0])])
+        wanted = wanted + jnp.where(slot == jnp.where(owned, filled, slots), panel * 32, 0)
+        filled = filled + owned.astype(jnp.int32)
+    return (row == wanted).astype(jnp.bfloat16)
+
+
+def product_kernel(slots, core_ref, owners_ref, got_ref, right_ref, right2_ref, out_ref, dense, lists, places, sem):
     sources = got_ref.shape[0]
     depth = right_ref.shape[0]
     core = core_ref[0]
     for source in range(sources):
-        lists[source * 8 : source * 8 + 8, :] = got_ref[source, PACKED_ROWS:, :].astype(jnp.int32)[:8]
+        lists[source : source + 1, :] = got_ref[source, PACKED_ROWS : PACKED_ROWS + 1, :].astype(jnp.int32)
     copy = pltpu.make_async_copy(lists, places, sem)
     copy.start()
     dense[...] = jnp.zeros_like(dense)
+    order = destination_order(owners_ref, slots)
     copy.wait()
-    lane = lax.broadcasted_iota(jnp.int32, (32, LANES), 1)
-
-    def one_source(source, too_many):
-        count = places[source * 8, 32]
-        first = jnp.where(source // 8 == core, 0, depth)
-        top = lax.rem(source, 8) * HALF
-
-        def one_block(slot, carry):
-            i = places[source * 8, slot]
-            j = places[source * 8, slot + 16]
-            block = got_ref[source, pl.ds(pl.multiple_of(lax.div(slot, 2) * 32, 32), 32), :]
+    side_of_lane = lax.broadcasted_iota(jnp.int32, (32, LANES), 1) // ATOM_BLOCK
+
+    def put(source, first, slots_here):
+        for slot in slots_here:
+            i = places[source, slot]
+            j = places[source, slot + 16]
+            block = got_ref[source, slot // 2 * 32 : slot // 2 * 32 + 32, :]
+            turned = pltpu.roll(block, ATOM_BLOCK, 1)
             side = lax.rem(j, 2)
-            placed = jnp.where(side == lax.rem(slot, 2), block, pltpu.roll(block, ATOM_BLOCK, 1))
-            to_rows = pl.ds(pl.multiple_of(top + i * 32, 32), 32)
+            placed = jnp.where(side == slot % 2, block, turned)
+            to_rows = pl.ds(pl.multiple_of(i * 256 + source % 8 * 32, 32), 32)
             to_lanes = pl.ds(pl.multiple_of(first + lax.div(j, 2) * LANES, LANES), LANES)
-            dense[to_rows, to_lanes] = jnp.where(lane // ATOM_BLOCK == side, placed, dense[to_rows, to_lanes])
-            return carry
-
-        lax.fori_loop(0, jnp.minimum(count, SLOTS), one_block, 0)
-        return jnp.logical_or(too_many, count > SLOTS)
-
-    too_many = lax.fori_loop(0, sources, one_source, jnp.bool_(False))
-    for m in range(0, out_ref.shape[0], 128):
-        out_ref[m : m + 128, :] = jnp.dot(
-            dense[m : m + 128, :depth], right_ref[...], preferred_element_type=jnp.float32
-        ) + jnp.dot(dense[m : m + 128, depth:], right2_ref[...], preferred_element_type=jnp.float32)
+            here = side_of_lane == jnp.where(slot < places[source, 32], side, 2)
+            dense[to_rows, to_lanes] = jnp.where(here, placed, dense[to_rows, to_lanes])
+
+    too_many = jnp.bool_(False)
+    for source in range(sources):
+        first = jnp.where(core == source // 8, 0, depth)
+        put(source, first, range(SLOTS // 2))
+
+        @pl.when(places[source, 32] > SLOTS // 2)
+        def _(source=source, first=first):
+            put(source, first, range(SLOTS // 2, SLOTS))
+
+        too_many = jnp.logical_or(too_many, places[source, 32] > SLOTS)
+
+    size = 32 * slots
+    for i in range(2):
+        rows = jnp.dot(order, dense[i * 256 : i * 256 + 256, :], preferred_element_type=jnp.float32).astype(jnp.bfloat16)
+        sums = jnp.dot(rows[:, :depth], right_ref[...], preferred_element_type=jnp.float32) + jnp.dot(
+            rows[:, depth:], right2_ref[...], preferred_element_type=jnp.float32
+        )
+        parts = sums.shape[1] // LANES
+        for q in range(parts):
+            out_ref[pl.ds(i * size * parts + q, size, stride=parts), :] = sums[:, q * LANES : (q + 1) * LANES]
 
     @pl.when(too_many)
     def _():
@@ -113,22 +141,22 @@
     )(marks, left)
 
 
-def unpack_product(core, got, right, right2):
+def unpack_product(slots, core, owners, got, right, right2):
     depth, width = right.shape
     return pl.pallas_call(
-        product_kernel,
-        out_shape=jax.ShapeDtypeStruct((8 * HALF, width), jnp.float32),
-        in_specs=[pl.BlockSpec(memory_space=pltpu.SMEM)] + [pl.BlockSpec(memory_space=pltpu.VMEM)] * 3,
+        functools.partial(product_kernel, slots),
+        out_shape=jax.ShapeDtypeStruct((32 * slots * 2 * (width // LANES), LANES), jnp.float32),
+        in_specs=[pl.BlockSpec(memory_space=pltpu.SMEM)] * 2 + [pl.BlockSpec(memory_space=pltpu.VMEM)] * 3,
         out_specs=pl.BlockSpec(memory_space=pltpu.VMEM),
         scratch_shapes=[
-            pltpu.VMEM((8 * HALF, 2 * depth), jnp.bfloat16),
-            pltpu.VMEM((16 * 8, LANES), jnp.int32),
-            pltpu.SMEM((16 * 8, LANES), jnp.int32),
+            pltpu.VMEM((512, 2 * depth), jnp.bfloat16),
+            pltpu.VMEM((16, LANES), jnp.int32),
+            pltpu.SMEM((16, LANES), jnp.int32),
             pltpu.SemaphoreType.DMA,
         ],
         compiler_params=pltpu.CompilerParams(vmem_limit_bytes=24 * 2**20),
-        cost_estimate=pl.CostEstimate(flops=2 * 8 * HALF * 2 * depth * width, bytes_accessed=4 * 2**20, transcendentals=0),
-    )(core.reshape(1), got, right, right2)
+        cost_estimate=pl.CostEstimate(flops=2 * 512 * 2 * depth * width, bytes_accessed=4 * 2**20, transcendentals=0),
+    )(core.reshape(1), owners, got, right, right2)
 
 
 def spread_marks(marks):
@@ -152,30 +180,48 @@
     )
 
 
-def reduce_rows(product):
+def reduce_dense(product):
     width = product.shape[-1]
     parts = (product * WIRE_SCALE).astype(WIRE).reshape(8, 32, 2, width).transpose(1, 0, 2, 3)
     got = lax.all_to_all(parts, ("zhi", "y"), 0, 0, tiled=True)
     return jnp.sum(got.astype(jnp.float32), axis=0) * (1.0 / WIRE_SCALE)
 
 
+def update(slab, chosen, sums):
+    picked = jnp.sum(jnp.where(chosen.reshape(chosen.shape + (1,) * (sums.ndim - 1)), sums[None], 0.0), axis=1)
+    return 1.5 * slab.astype(jnp.float32) - 0.5 * picked.reshape(slab.shape)
+
+
 def body(left, right, occupancy, owners, slab):
     core = lax.axis_index("core")
+    panels = jnp.arange(8)
 
     right2 = lax.ppermute(right, "core", [(0, 1), (1, 0)])
-
-    got = lax.all_to_all(pack(occupancy, left), ("core", "zlo", "x"), 0, 0, tiled=True)
-    summed = reduce_rows(unpack_product(core, got, right, right2))
-
-    summed = lax.cond(
-        jnp.isnan(summed[0, 0, 0]),
-        lambda: reduce_rows(dense_product(core, left, right, right2, occupancy)),
-        lambda: summed,
+    packed, owners = lax.optimization_barrier((pack(occupancy, left), owners))
+    got = lax.all_to_all(packed, ("core", "zlo", "x"), 0, 0, tiled=True)
+
+    owned = jnp.any(owners[:, None] == panels[None, :], axis=0)
+    number = jnp.sum(owned)
+    slot_of_step = jnp.sum(owned[None, :] & (panels[None, :] < owners[:, None]), axis=1)
+
+    def reduced(slots):
+        def branch():
+            product = unpack_product(slots, core, owners, got, right, right2)
+            parts = (product * WIRE_SCALE).astype(WIRE).reshape(32, slots, TILE, LANES)
+            came = lax.all_to_all(parts, ("zhi", "y"), 0, 0, tiled=True)
+            sums = jnp.sum(came.astype(jnp.float32), axis=0) * (1.0 / WIRE_SCALE)
+            return update(slab, slot_of_step[:, None] == jnp.arange(slots)[None, :], sums)
+
+        return branch
+
+    which = sum((number > slots).astype(jnp.int32) for slots in DISTINCT[:-1])
+    updated = lax.switch(which, [reduced(slots) for slots in DISTINCT])
+
+    return lax.cond(
+        jnp.isnan(updated[0, 0, 0]),
+        lambda: update(slab, owners[:, None] == panels[None, :], reduce_dense(dense_product(core, left, right, right2, occupancy))),
+        lambda: updated,
     )
-
-    chosen = owners[:, None] == jnp.arange(8)[None, :]
-    picked = jnp.sum(jnp.where(chosen[:, :, None, None], summed[None], 0.0), axis=1)
-    return 1.5 * slab.astype(jnp.float32) - 0.5 * picked
 
 
 def solution(mesh):

time: 66.6 us -> 61.2 us (0.919)
  waiting for transfers between devices: 29.6 us -> 23.9 us
  between operations: 1.4 us -> 3.34 us
  local copies, waits for them, and re-layouts: 2.72 us -> 1.16 us
  Pallas kernels: 7.53 us -> 6.33 us
    all_to_all x2, waiting for transfers between devices: 27.7 us -> 23.9 us  [the longest x1 17.7 us: branch(): came = lax.all_to_all(parts, ('zhi', 'y'), 0, 0, tiled=True)]
    ppermute x1, waiting for transfers between devices: 1.89 us -> 0.01 us  [body(): right2 = lax.ppermute(right, 'core', [(0, 1), (1, 0)])]
    reshape x2 -> x0, local copies, waits for them, and re-layouts: 1.61 us -> none  [reduce_rows(): (product * WIRE_SCALE).astype(WIRE).reshape(8, 32, 2, width)]
    pallas_call x1, Pallas kernels: 5.03 us -> 3.9 us  [unpack_product(): pl.pallas_call(functools.partial(product_kernel, slots), out_shape=jax.Sh...]
    convert_element_type x1 -> x2, other arithmetic: 0.13 us -> 0.89 us  [the longest x1 0.82 us: branch(): parts = (product * WIRE_SCALE).astype(WIRE).reshape(32, slots, TILE, LANES)]
  transfers between devices with their start and end apart: 3 -> 3, of which waited for: 3 -> 2; matrix products, arithmetic and copies ran while one was open for 0% -> 2% of each run, Pallas kernels for 0% -> 0%
where the time goes in v5:
time: 61.2 us; the launch traced here: 60.8 us
  waiting for transfers between devices  23.9 us (39%)
  starting transfers between devices  23.8 us (39%)
  Pallas kernels  6.33 us (10%)
  between operations  3.34 us (5%)
  other arithmetic  2.03 us (3%)
  local copies, waits for them, and re-layouts  1.16 us (2%)
    all_to_all x1, waiting for transfers between devices, branch(): came = lax.all_to_all(parts, ('zhi', 'y'), 0, 0, tiled=True)  17.7 us
    all_to_all x1, starting transfers between devices, branch(): came = lax.all_to_all(parts, ('zhi', 'y'), 0, 0, tiled=True)  15.3 us
    all_to_all x1, waiting for transfers between devices, body(): got = lax.all_to_all(packed, ('core', 'zlo', 'x'), 0, 0, tiled=True)  6.27 us
    all_to_all x1, starting transfers between devices, body(): got = lax.all_to_all(packed, ('core', 'zlo', 'x'), 0, 0, tiled=True)  6.15 us
    pallas_call x1, Pallas kernels, unpack_product(): pl.pallas_call(functools.partial(product_kernel, slots), out_shape=jax.Sh...  3.9 us
    pallas_call x1, Pallas kernels, pack(): pl.pallas_call(pack_kernel, out_shape=jax.ShapeDtypeStruct((16, PACKED_RO...  2.43 us
    ppermute x1, starting transfers between devices, body(): right2 = lax.ppermute(right, 'core', [(0, 1), (1, 0)])  2.32 us
  transfers between devices with their start and end apart: 3, of which 2 were waited for; matrix products, arithmetic and copies ran while one was open for 2% of the time, Pallas kernels for 0%

profile of v5, /device:TPU:8, one launch (start us, length us, event | category | flops | bytes accessed | tf_op | source)
XLA Modules:
  0.0 60.8 jit_solution(3037760881114999550)
XLA Ops:
  0.0 0.0 copy-start.4
  0.0 0.0 copy-start
  0.0 0.0 copy-start.2
  0.0 2.4 %shard_map.57 = bf16[16,144,128]{2,1,0:T(8,128)(2,1)} custom-call(s32[2,12]{1,0:T(2,128)} %marks_ref.1, bf16[128,768]{1,0:T(8,128)(2,1)} %left_ref.1), custom_call_target="tpu_custom_call" | custom-call | tf_op jit(solution)/shard_map/pallas_call | solution.py:132
  2.4 6.1 %all-to-all-start.6 = ((bf16[16,144,128]{2,1,0:T(8,128)(2,1)}), bf16[16,144,128]{2,1,0:T(8,128)(2,1)S(1)}, u32[]{:S(2)}, u32[]{:S(2)}) async-start(bf16[16,144,128]{2,1,0:T(8,128)(2,1)} %shard_map.57), calls=%async_computation.6 | async-start | bytes 1179648 | tf_op jit(solution)/shard_map/all_to_all | solution.py:201
  8.6 0.0 copy-done
  8.6 2.3 %collective-permute-start = (bf16[768,512]{1,0:T(8,128)(2,1)S(1)}, bf16[768,512]{1,0:T(8,128)(2,1)S(1)}, u32[]{:S(2)}, u32[]{:S(2)}) collective-permute-start(bf16[768,512]{1,0:T(8,128)(2,1)S(1)} %copy-done), channel_id=1, source_target_pairs={{0,8},{8,0},{1,9},{9,1},{2,10},{10,2},{3,11},{11,3},{4,12},{12,4},... | collective-permute-start | bytes 2359304 | tf_op jit(solution)/shard_map/ppermute | solution.py:199
  10.9 0.0 copy-done.4
  10.9 0.1 fusion.41
  11.0 0.6 %convert_reduce_fusion.5 = s32[]{:T(128)} fusion(pred[8]{0:T(512)(128)(4,1)S(1)} %fusion.41), kind=kLoop, calls=%fused_computation.96 | loop fusion | flops 15 | bytes 12 | tf_op jit(solution)/shard_map/reduce_sum | solution.py:204
  13.6 0.1 fusion.43
  13.7 0.0 collective-permute-done
  13.7 6.3 %all-to-all-done.6 = bf16[16,144,128]{2,1,0:T(8,128)(2,1)S(1)} async-done(((bf16[16,144,128]{2,1,0:T(8,128)(2,1)}), bf16[16,144,128]{2,1,0:T(8,128)(2,1)S(1)}, u32[]{:S(2)}, u32[]{:S(2)}) %all-to-all-start.6) | async-done | bytes 589856 | tf_op jit(solution)/shard_map/all_to_all | solution.py:201
  20.0 0.0 copy-done.2
  20.0 0.0 copy-start.1
  20.0 0.0 copy-start.5
  20.0 38.4 %conditional.2 = (f32[8,2,512]{2,1,0:T(2,128)S(1)}) conditional(s32[]{:T(128)} %clamp.3, (bf16[8,2,512]{2,1,0:T(2,128)(2,1)S(1)}, s32[8,8]{1,0:T(8,128)S(1)}, s32[]{:T(128)}, s32[8]{0:T(128)S(1)}, bf16[16,144,128]{2,1,0:T(8,128)(2,1)S(1)}, /*index=5*/bf16[768,512]{1,0:T(8,128)(2,1)S(1)}, ...), branch_computations={%region_3.6_spmd, %region_6.9_spmd, %region_9.12_spmd, %region_12.... | conditional | flops 806510720 | bytes 8241644 | solution.py:218
  20.0 3.9 %branch_2_fun.1 = f32[1536,128]{1,0:T(8,128)S(1)} custom-call(s32[1]{0:T(128)} %bitcast.4.core_ref, s32[8]{0:T(128)S(1)} %get-tuple-element.103.owners_ref, bf16[16,144,128]{2,1,0:T(8,128)(2,1)S(1)} %get-tuple-element.104.got_ref, bf16[768,512]{1,0:T(8,128)(2,1)S(1)} %get-tuple-element.105.right_ref, bf16[768,512]{1,0:T(8,128)(2,1)S(1)} %get-tuple-element.106.right2_ref), custom_call_target="tpu_custom_call" | custom-call | flops 805306368 | bytes 4194304 | tf_op jit(solution)/shard_map/cond/branch_2_fun/pallas_call | solution.py:146
  23.9 0.8 %multiply_convert_fusion.2 = f16[1536,128]{1,0:T(8,128)(2,1)} fusion(f32[1536,128]{1,0:T(8,128)S(1)} %branch_2_fun.1), kind=kLoop, calls=%fused_computation.78 | loop fusion | flops 393216 | bytes 1179648 | tf_op jit(solution)/shard_map/cond/branch_2_fun/convert_element_type | solution.py:210
  24.7 15.3 %all-to-all-start.2 = ((f16[32,6,8,128]{3,2,1,0:T(8,128)(2,1)}), f16[32,6,8,128]{3,2,1,0:T(8,128)(2,1)S(1)}, u32[]{:S(2)}, u32[]{:S(2)}) async-start(f16[32,6,8,128]{3,2,1,0:T(8,128)(2,1)} %bitcast.5), calls=%async_computation.2 | async-start | bytes 786432 | tf_op jit(solution)/shard_map/cond/branch_2_fun/all_to_all | solution.py:211
  40.0 0.1 reduce_sum.112
  40.2 0.1 iota_compare_fusion.2
  40.2 17.7 %all-to-all-done.2 = f16[32,6,8,128]{3,2,1,0:T(8,128)(2,1)S(1)} async-done(((f16[32,6,8,128]{3,2,1,0:T(8,128)(2,1)}), f16[32,6,8,128]{3,2,1,0:T(8,128)(2,1)S(1)}, u32[]{:S(2)}, u32[]{:S(2)}) %all-to-all-start.2) | async-done | bytes 393248 | tf_op jit(solution)/shard_map/cond/branch_2_fun/all_to_all | solution.py:211
  57.9 0.1 convert_reduce_fusion.3
  58.0 0.1 select_reduce_fusion.3
  58.4 0.5 slice.4
  60.2 0.0 copy-done.1
  60.2 0.0 copy-done.5
  60.2 0.0 copy-start.3
  60.2 0.6 copy-done.3
  (6 shorter events, 0.1 us)
Async XLA Ops:
  0.0 10.9 %copy-start.4 = (s32[8]{0:T(128)S(1)}, s32[8]{0:T(128)}, u32[]{:S(2)}) copy-start(s32[8]{0:T(128)} %param.14) | copy-start | bytes 100
  0.0 8.6 %copy-start = (bf16[768,512]{1,0:T(8,128)(2,1)S(1)}, bf16[768,512]{1,0:T(8,128)(2,1)}, u32[]{:S(2)}) copy-start(bf16[768,512]{1,0:T(8,128)(2,1)} %param.12) | copy-start | bytes 2359300
  0.0 20.0 %copy-start.2 = (bf16[8,2,512]{2,1,0:T(2,128)(2,1)S(1)}, bf16[8,2,512]{2,1,0:T(2,128)(2,1)}, u32[]{:S(2)}) copy-start(bf16[8,2,512]{2,1,0:T(2,128)(2,1)} %param.15) | copy-start | bytes 49156
  2.4 17.5 %all-to-all-start.6 = ((bf16[16,144,128]{2,1,0:T(8,128)(2,1)}), bf16[16,144,128]{2,1,0:T(8,128)(2,1)S(1)}, u32[]{:S(2)}, u32[]{:S(2)}) async-start(bf16[16,144,128]{2,1,0:T(8,128)(2,1)} %shard_map.57), calls=%async_computation.6 | async-start | bytes 1179648 | tf_op jit(solution)/shard_map/all_to_all | solution.py:201
  8.6 5.1 %collective-permute-start = (bf16[768,512]{1,0:T(8,128)(2,1)S(1)}, bf16[768,512]{1,0:T(8,128)(2,1)S(1)}, u32[]{:S(2)}, u32[]{:S(2)}) collective-permute-start(bf16[768,512]{1,0:T(8,128)(2,1)S(1)} %copy-done), channel_id=1, source_target_pairs={{0,8},{8,0},{1,9},{9,1},{2,10},{10,2},{3,11},{11,3},{4,12},{12,4},... | collective-permute-start | bytes 2359304 | tf_op jit(solution)/shard_map/ppermute | solution.py:199
  20.0 40.2 %copy-start.1 = (bf16[128,768]{1,0:T(8,128)(2,1)S(1)}, bf16[128,768]{1,0:T(8,128)(2,1)}, u32[]{:S(2)}) copy-start(bf16[128,768]{1,0:T(8,128)(2,1)} %left_ref.1) | copy-start | bytes 589828
  20.0 40.2 %copy-start.5 = (s32[2,12]{1,0:T(2,128)S(1)}, s32[2,12]{1,0:T(2,128)}, u32[]{:S(2)}) copy-start(s32[2,12]{1,0:T(2,128)} %marks_ref.1) | copy-start | bytes 292
  24.7 33.2 %all-to-all-start.2 = ((f16[32,6,8,128]{3,2,1,0:T(8,128)(2,1)}), f16[32,6,8,128]{3,2,1,0:T(8,128)(2,1)S(1)}, u32[]{:S(2)}, u32[]{:S(2)}) async-start(f16[32,6,8,128]{3,2,1,0:T(8,128)(2,1)} %bitcast.5), calls=%async_computation.2 | async-start | bytes 786432 | tf_op jit(solution)/shard_map/cond/branch_2_fun/all_to_all | solution.py:211
  60.2 0.6 %copy-start.3 = (f32[8,2,512]{2,1,0:T(2,128)}, f32[8,2,512]{2,1,0:T(2,128)S(1)}, u32[]{:S(2)}) copy-start(f32[8,2,512]{2,1,0:T(2,128)S(1)} %get-tuple-element.197) | copy-start | bytes 98308

commit v6 on v5

--- a/solution.py
+++ b/solution.py
@@ -13,7 +13,7 @@
 SLOTS = 8
 LANES = 128
 TILE = 8
-DISTINCT = (4, 5, 6, 8)
+DISTINCT = (3, 4, 5, 6, 7, 8)
 PACKED_ROWS = SLOTS // 2 * 32
 LIST_ROWS = 16
 WIRE = jnp.float16
@@ -63,20 +63,20 @@
 
 
 def destination_order(owners_ref, slots):
-    shape = (32 * slots, 256)
-    place = lax.broadcasted_iota(jnp.int32, shape, 0)
-    row = lax.broadcasted_iota(jnp.int32, shape, 1)
-    at, slot, b = place // (2 * slots), place // 2 % slots, place % 2
+    place = lax.broadcasted_iota(jnp.int32, (32 * slots, 1), 0)
+    at = sum((place >= k * 2 * slots).astype(jnp.int32) for k in range(1, 16))
+    slot, b = (place - at * (2 * slots)) // 2, place % 2
     wanted = at * 2 + b
     filled = jnp.int32(0)
     for panel in range(8):
         owned = functools.reduce(jnp.logical_or, [owners_ref[t] == panel for t in range(owners_ref.shape[0])])
         wanted = wanted + jnp.where(slot == jnp.where(owned, filled, slots), panel * 32, 0)
         filled = filled + owned.astype(jnp.int32)
+    row = lax.broadcasted_iota(jnp.int32, (32 * slots, 256), 1)
     return (row == wanted).astype(jnp.bfloat16)
 
 
-def product_kernel(slots, core_ref, owners_ref, got_ref, right_ref, right2_ref, out_ref, dense, lists, places, sem):
+def product_kernel(slots, core_ref, owners_ref, got_ref, right_ref, right2_ref, out_ref, flag_ref, dense, lists, places, sem):
     sources = got_ref.shape[0]
     depth = right_ref.shape[0]
     core = core_ref[0]
@@ -102,16 +102,18 @@
             here = side_of_lane == jnp.where(slot < places[source, 32], side, 2)
             dense[to_rows, to_lanes] = jnp.where(here, placed, dense[to_rows, to_lanes])
 
-    too_many = jnp.bool_(False)
+    firsts = [jnp.where(core == source // 8, 0, depth) for source in range(sources)]
     for source in range(sources):
-        first = jnp.where(core == source // 8, 0, depth)
-        put(source, first, range(SLOTS // 2))
+        put(source, firsts[source], range(SLOTS // 2))
+    most = jnp.int32(0)
+    for source in range(sources):
+        most = jnp.maximum(most, places[source, 32])
 
         @pl.when(places[source, 32] > SLOTS // 2)
-        def _(source=source, first=first):
-            put(source, first, range(SLOTS // 2, SLOTS))
-
-        too_many = jnp.logical_or(too_many, places[source, 32] > SLOTS)
+        def _(source=source):
+            put(source, firsts[source], range(SLOTS // 2, SLOTS))
+
+    flag_ref[0] = (most > SLOTS).astype(jnp.int32)
 
     size = 32 * slots
     for i in range(2):
@@ -122,10 +124,6 @@
         parts = sums.shape[1] // LANES
         for q in range(parts):
             out_ref[pl.ds(i * size * parts + q, size, stride=parts), :] = sums[:, q * LANES : (q + 1) * LANES]
-
-    @pl.when(too_many)
-    def _():
-        out_ref[...] = jnp.full(out_ref.shape, jnp.nan, jnp.float32)
 
 
 def pack(marks, left):
@@ -145,9 +143,12 @@
     depth, width = right.shape
     return pl.pallas_call(
         functools.partial(product_kernel, slots),
-        out_shape=jax.ShapeDtypeStruct((32 * slots * 2 * (width // LANES), LANES), jnp.float32),
+        out_shape=[
+            jax.ShapeDtypeStruct((32 * slots * 2 * (width // LANES), LANES), jnp.float32),
+            jax.ShapeDtypeStruct((1,), jnp.int32),
+        ],
         in_specs=[pl.BlockSpec(memory_space=pltpu.SMEM)] * 2 + [pl.BlockSpec(memory_space=pltpu.VMEM)] * 3,
-        out_specs=pl.BlockSpec(memory_space=pltpu.VMEM),
+        out_specs=[pl.BlockSpec(memory_space=pltpu.VMEM), pl.BlockSpec(memory_space=pltpu.SMEM)],
         scratch_shapes=[
             pltpu.VMEM((512, 2 * depth), jnp.bfloat16),
             pltpu.VMEM((16, LANES), jnp.int32),
@@ -167,24 +168,23 @@
     ).reshape(count_r * ATOM_BLOCK, count_c * ATOM_BLOCK)
 
 
-def dense_product(core, left, right, right2, occupancy):
-    depth = right.shape[0]
+def dense_product(slots, core, owners, left, right, right2, occupancy):
+    depth, width = right.shape
     kept = left * spread_marks(occupancy)
     halves = jnp.dot(row_order(), kept, preferred_element_type=jnp.float32).astype(jnp.bfloat16)
     sent = jnp.broadcast_to(halves.reshape(2, 1, HALF, depth), (2, 8, HALF, depth)).reshape(16, HALF, depth)
     panels = lax.all_to_all(sent, ("core", "zlo", "x"), 0, 0, tiled=True).reshape(2, 8 * HALF, depth)
     own = lax.dynamic_index_in_dim(panels, core, 0, keepdims=False)
     other = lax.dynamic_index_in_dim(panels, 1 - core, 0, keepdims=False)
-    return jnp.dot(own, right, preferred_element_type=jnp.float32) + jnp.dot(
+    product = jnp.dot(own, right, preferred_element_type=jnp.float32) + jnp.dot(
         other, right2, preferred_element_type=jnp.float32
     )
-
-
-def reduce_dense(product):
-    width = product.shape[-1]
-    parts = (product * WIRE_SCALE).astype(WIRE).reshape(8, 32, 2, width).transpose(1, 0, 2, 3)
-    got = lax.all_to_all(parts, ("zhi", "y"), 0, 0, tiled=True)
-    return jnp.sum(got.astype(jnp.float32), axis=0) * (1.0 / WIRE_SCALE)
+    number = jnp.arange(8)
+    owned = jnp.any(owners[:, None] == number[None, :], axis=0)
+    before = jnp.sum(owned[:, None] & (number[:, None] < number[None, :]), axis=0)
+    panel_of_slot = jnp.sum(jnp.where(owned[None, :] & (before[None, :] == number[:slots, None]), number[None, :], 0), axis=1)
+    chosen = jnp.take(product.reshape(8, 32, 2 * width // LANES, LANES), panel_of_slot, axis=0)
+    return chosen.transpose(1, 0, 2, 3).reshape(-1, LANES)
 
 
 def update(slab, chosen, sums):
@@ -206,7 +206,11 @@
 
     def reduced(slots):
         def branch():
-            product = unpack_product(slots, core, owners, got, right, right2)
+            product, flag = unpack_product(slots, core, owners, got, right, right2)
+            product = lax.switch(
+                flag[0],
+                [lambda: product, lambda: dense_product(slots, core, owners, left, right, right2, occupancy)],
+            )
             parts = (product * WIRE_SCALE).astype(WIRE).reshape(32, slots, TILE, LANES)
             came = lax.all_to_all(parts, ("zhi", "y"), 0, 0, tiled=True)
             sums = jnp.sum(came.astype(jnp.float32), axis=0) * (1.0 / WIRE_SCALE)
@@ -215,13 +219,7 @@
         return branch
 
     which = sum((number > slots).astype(jnp.int32) for slots in DISTINCT[:-1])
-    updated = lax.switch(which, [reduced(slots) for slots in DISTINCT])
-
-    return lax.cond(
-        jnp.isnan(updated[0, 0, 0]),
-        lambda: update(slab, owners[:, None] == panels[None, :], reduce_dense(dense_product(core, left, right, right2, occupancy))),
-        lambda: updated,
-    )
+    return lax.switch(which, [reduced(slots) for slots in DISTINCT])
 
 
 def solution(mesh):

time: 61.2 us -> 59.9 us (0.979)
  waiting for transfers between devices: 23.9 us -> 21.3 us
  loops' own time: 0.24 us -> 1.19 us
    all_to_all x1, waiting for transfers between devices: 17.7 us -> 16.3 us  [branch(): came = lax.all_to_all(parts, ('zhi', 'y'), 0, 0, tiled=True)]
    all_to_all x1, waiting for transfers between devices: 6.27 us -> 4.98 us  [body(): got = lax.all_to_all(packed, ('core', 'zlo', 'x'), 0, 0, tiled=True)]
    another operation x2, loops' own time: 0.24 us -> 1.19 us  [the longest x1 1.18 us: body(): return lax.switch(which, [reduced(slots) for slots in DISTINCT])]
    cond x0 -> x2, local copies, waits for them, and re-layouts: none -> 0.8 us
where the time goes in v6:
time: 59.9 us; the launch traced here: 59.5 us
  starting transfers between devices  23.8 us (40%)
  waiting for transfers between devices  21.3 us (36%)
  Pallas kernels  6.42 us (11%)
  between operations  3.33 us (6%)
  other arithmetic  1.97 us (3%)
  local copies, waits for them, and re-layouts  1.45 us (2%)
  loops' own time  1.19 us (2%)
    all_to_all x1, waiting for transfers between devices, branch(): came = lax.all_to_all(parts, ('zhi', 'y'), 0, 0, tiled=True)  16.3 us
    all_to_all x1, starting transfers between devices, branch(): came = lax.all_to_all(parts, ('zhi', 'y'), 0, 0, tiled=True)  15 us
    all_to_all x1, starting transfers between devices, body(): got = lax.all_to_all(packed, ('core', 'zlo', 'x'), 0, 0, tiled=True)  6.48 us
    all_to_all x1, waiting for transfers between devices, body(): got = lax.all_to_all(packed, ('core', 'zlo', 'x'), 0, 0, tiled=True)  4.98 us
    pallas_call x1, Pallas kernels, unpack_product(): pl.pallas_call(functools.partial(product_kernel, slots), out_shape=[jax.S...  4.11 us
    ppermute x1, starting transfers between devices, body(): right2 = lax.ppermute(right, 'core', [(0, 1), (1, 0)])  2.32 us
    pallas_call x1, Pallas kernels, pack(): pl.pallas_call(pack_kernel, out_shape=jax.ShapeDtypeStruct((16, PACKED_RO...  2.32 us
  transfers between devices with their start and end apart: 3, of which 2 were waited for; matrix products, arithmetic and copies ran while one was open for 2% of the time, Pallas kernels for 0%

profile of v6, /device:TPU:8, one launch (start us, length us, event | category | flops | bytes accessed | tf_op | source)
XLA Modules:
  0.0 59.5 jit_solution(13960002577236932280)
XLA Ops:
  0.0 0.0 copy-start.7
  0.0 0.0 copy-start.1
  0.0 0.0 copy-start.9
  0.0 0.0 copy-start
  0.0 0.0 copy-start.2
  0.0 2.3 %shard_map.67 = bf16[16,144,128]{2,1,0:T(8,128)(2,1)} custom-call(s32[2,12]{1,0:T(2,128)} %marks_ref.1, bf16[128,768]{1,0:T(8,128)(2,1)} %left_ref.1), custom_call_target="tpu_custom_call" | custom-call | tf_op jit(solution)/shard_map/pallas_call | solution.py:130
  2.3 6.5 %all-to-all-start.12 = ((bf16[16,144,128]{2,1,0:T(8,128)(2,1)}), bf16[16,144,128]{2,1,0:T(8,128)(2,1)S(1)}, u32[]{:S(2)}, u32[]{:S(2)}) async-start(bf16[16,144,128]{2,1,0:T(8,128)(2,1)} %shard_map.67), calls=%async_computation.12 | async-start | bytes 1179648 | tf_op jit(solution)/shard_map/all_to_all | solution.py:201
  8.8 0.0 copy-done
  8.8 2.3 %collective-permute-start = (bf16[768,512]{1,0:T(8,128)(2,1)S(1)}, bf16[768,512]{1,0:T(8,128)(2,1)S(1)}, u32[]{:S(2)}, u32[]{:S(2)}) collective-permute-start(bf16[768,512]{1,0:T(8,128)(2,1)S(1)} %copy-done), channel_id=1, source_target_pairs={{0,8},{8,0},{1,9},{9,1},{2,10},{10,2},{3,11},{11,3},{4,12},{12,4},... | collective-permute-start | bytes 2359304 | tf_op jit(solution)/shard_map/ppermute | solution.py:199
  11.2 0.0 copy-done.9
  11.2 0.1 fusion.253
  11.3 0.6 %convert_reduce_fusion.12 = s32[]{:T(128)} fusion(pred[8]{0:T(512)(128)(4,1)S(1)} %fusion.253), kind=kLoop, calls=%fused_computation.457 | loop fusion | flops 15 | bytes 12 | tf_op jit(solution)/shard_map/reduce_sum | solution.py:204
  15.1 0.1 fusion.255
  15.2 0.0 collective-permute-done
  15.2 5.0 %all-to-all-done.12 = bf16[16,144,128]{2,1,0:T(8,128)(2,1)S(1)} async-done(((bf16[16,144,128]{2,1,0:T(8,128)(2,1)}), bf16[16,144,128]{2,1,0:T(8,128)(2,1)S(1)}, u32[]{:S(2)}, u32[]{:S(2)}) %all-to-all-start.12) | async-done | bytes 589856 | tf_op jit(solution)/shard_map/all_to_all | solution.py:201
  20.2 0.0 copy-done.7
  20.2 0.0 copy-done.1
  20.2 0.0 copy-done.2
  20.2 38.6 %conditional.7 = (f32[8,2,512]{2,1,0:T(2,128)S(1)}) conditional(s32[]{:T(128)} %clamp.39, (bf16[8,2,512]{2,1,0:T(2,128)(2,1)S(1)}, s32[8,8]{1,0:T(8,128)S(1)}, s32[]{:T(128)}, s32[8]{0:T(128)S(1)}, bf16[16,144,128]{2,1,0:T(8,128)(2,1)S(1)}, /*index=5*/bf16[768,512]{1,0:T(8,128)(2,1)S(1)}, ...), branch_computations={%region_3.11_spmd, %region_11.19_spmd, %region_19.27_spmd, %region... | conditional | flops 1638085120 | bytes 33353872 | solution.py:222
  20.2 0.0 copy-start.3
  20.3 0.8 %copy-done.3 = bf16[16,144,128]{2,1,0:T(8,128)(2,1)} copy-done((bf16[16,144,128]{2,1,0:T(8,128)(2,1)}, bf16[16,144,128]{2,1,0:T(8,128)(2,1)S(1)}, u32[]{:S(2)}) %copy-start.3) | copy-done | bytes 589848 | tf_op jit(solution)/shard_map/cond
  21.1 4.1 %branch_2_fun.1 = (f32[1280,128]{1,0:T(8,128)S(1)}, s32[1]{0:T(128)}) custom-call(s32[1]{0:T(128)} %bitcast.33.core_ref, s32[8]{0:T(128)S(1)} %get-tuple-element.259.owners_ref, bf16[16,144,128]{2,1,0:T(8,128)(2,1)} %copy-done.3, bf16[768,512]{1,0:T(8,128)(2,1)S(1)} %get-tuple-element.261.right_ref, bf16[768,512]{1,0:T(8,128)(2,1)S(1)} %get-tuple-element.262.right2_ref), custom_call_target="tpu_custom_call" | custom-call | flops 805306368 | bytes 4194304 | tf_op jit(solution)/shard_map/cond/branch_2_fun/pallas_call | solution.py:144
  25.8 0.8 %multiply_convert_fusion.2 = f16[1280,128]{1,0:T(8,128)(2,1)} fusion(f32[1280,128]{1,0:T(8,128)S(1)} %get-tuple-element.535), kind=kLoop, calls=%fused_computation.222 | loop fusion | flops 327680 | bytes 983040 | tf_op jit(solution)/shard_map/cond/branch_2_fun/convert_element_type | solution.py:214
  26.5 15.0 %all-to-all-start.5 = ((f16[32,5,8,128]{3,2,1,0:T(8,128)(2,1)}), f16[32,5,8,128]{3,2,1,0:T(8,128)(2,1)S(1)}, u32[]{:S(2)}, u32[]{:S(2)}) async-start(f16[32,5,8,128]{3,2,1,0:T(8,128)(2,1)} %bitcast.35), calls=%async_computation.5 | async-start | bytes 655360 | tf_op jit(solution)/shard_map/cond/branch_2_fun/all_to_all | solution.py:215
  41.5 0.1 reduce_sum.250
  41.7 0.1 iota_compare_fusion.8
  41.7 16.3 %all-to-all-done.5 = f16[32,5,8,128]{3,2,1,0:T(8,128)(2,1)S(1)} async-done(((f16[32,5,8,128]{3,2,1,0:T(8,128)(2,1)}), f16[32,5,8,128]{3,2,1,0:T(8,128)(2,1)S(1)}, u32[]{:S(2)}, u32[]{:S(2)}) %all-to-all-start.5) | async-done | bytes 327712 | tf_op jit(solution)/shard_map/cond/branch_2_fun/all_to_all | solution.py:215
  58.1 0.1 convert_reduce_fusion.5
  58.1 0.1 select_reduce_fusion.5
  58.9 0.0 copy-start.8
  58.9 0.6 %copy-done.8 = f32[8,2,512]{2,1,0:T(2,128)} copy-done((f32[8,2,512]{2,1,0:T(2,128)}, f32[8,2,512]{2,1,0:T(2,128)S(1)}, u32[]{:S(2)}) %copy-start.8) | copy-done | bytes 32792
  (5 shorter events, 0.1 us)
Async XLA Ops:
  0.0 20.2 %copy-start.7 = (s32[2,12]{1,0:T(2,128)S(1)}, s32[2,12]{1,0:T(2,128)}, u32[]{:S(2)}) copy-start(s32[2,12]{1,0:T(2,128)} %marks_ref.1) | copy-start | bytes 292
  0.0 20.2 %copy-start.1 = (bf16[128,768]{1,0:T(8,128)(2,1)S(1)}, bf16[128,768]{1,0:T(8,128)(2,1)}, u32[]{:S(2)}) copy-start(bf16[128,768]{1,0:T(8,128)(2,1)} %left_ref.1) | copy-start | bytes 589828
  0.0 11.2 %copy-start.9 = (s32[8]{0:T(128)S(1)}, s32[8]{0:T(128)}, u32[]{:S(2)}) copy-start(s32[8]{0:T(128)} %param.26) | copy-start | bytes 100
  0.0 8.8 %copy-start = (bf16[768,512]{1,0:T(8,128)(2,1)S(1)}, bf16[768,512]{1,0:T(8,128)(2,1)}, u32[]{:S(2)}) copy-start(bf16[768,512]{1,0:T(8,128)(2,1)} %param.24) | copy-start | bytes 2359300
  0.0 20.2 %copy-start.2 = (bf16[8,2,512]{2,1,0:T(2,128)(2,1)S(1)}, bf16[8,2,512]{2,1,0:T(2,128)(2,1)}, u32[]{:S(2)}) copy-start(bf16[8,2,512]{2,1,0:T(2,128)(2,1)} %param.27) | copy-start | bytes 49156
  2.3 17.9 %all-to-all-start.12 = ((bf16[16,144,128]{2,1,0:T(8,128)(2,1)}), bf16[16,144,128]{2,1,0:T(8,128)(2,1)S(1)}, u32[]{:S(2)}, u32[]{:S(2)}) async-start(bf16[16,144,128]{2,1,0:T(8,128)(2,1)} %shard_map.67), calls=%async_computation.12 | async-start | bytes 1179648 | tf_op jit(solution)/shard_map/all_to_all | solution.py:201
  8.8 6.4 %collective-permute-start = (bf16[768,512]{1,0:T(8,128)(2,1)S(1)}, bf16[768,512]{1,0:T(8,128)(2,1)S(1)}, u32[]{:S(2)}, u32[]{:S(2)}) collective-permute-start(bf16[768,512]{1,0:T(8,128)(2,1)S(1)} %copy-done), channel_id=1, source_target_pairs={{0,8},{8,0},{1,9},{9,1},{2,10},{10,2},{3,11},{11,3},{4,12},{12,4},... | collective-permute-start | bytes 2359304 | tf_op jit(solution)/shard_map/ppermute | solution.py:199
  20.2 0.8 %copy-start.3 = (bf16[16,144,128]{2,1,0:T(8,128)(2,1)}, bf16[16,144,128]{2,1,0:T(8,128)(2,1)S(1)}, u32[]{:S(2)}) copy-start(bf16[16,144,128]{2,1,0:T(8,128)(2,1)S(1)} %get-tuple-element.260.got_ref) | copy-start | bytes 1769476 | tf_op jit(solution)/shard_map/cond
  26.5 31.5 %all-to-all-start.5 = ((f16[32,5,8,128]{3,2,1,0:T(8,128)(2,1)}), f16[32,5,8,128]{3,2,1,0:T(8,128)(2,1)S(1)}, u32[]{:S(2)}, u32[]{:S(2)}) async-start(f16[32,5,8,128]{3,2,1,0:T(8,128)(2,1)} %bitcast.35), calls=%async_computation.5 | async-start | bytes 655360 | tf_op jit(solution)/shard_map/cond/branch_2_fun/all_to_all | solution.py:215
  58.9 0.6 %copy-start.8 = (f32[8,2,512]{2,1,0:T(2,128)}, f32[8,2,512]{2,1,0:T(2,128)S(1)}, u32[]{:S(2)}) copy-start(f32[8,2,512]{2,1,0:T(2,128)S(1)} %get-tuple-element.556) | copy-start | bytes 98308

commit v7 on v6

--- a/solution.py
+++ b/solution.py
@@ -76,7 +76,7 @@
     return (row == wanted).astype(jnp.bfloat16)
 
 
-def product_kernel(slots, core_ref, owners_ref, got_ref, right_ref, right2_ref, out_ref, flag_ref, dense, lists, places, sem):
+def product_kernel(slots, core_ref, owners_ref, got_ref, right_ref, right2_ref, out_ref, flag_ref, dense, ordered, lists, places, sem):
     sources = got_ref.shape[0]
     depth = right_ref.shape[0]
     core = core_ref[0]
@@ -117,13 +117,15 @@
 
     size = 32 * slots
     for i in range(2):
-        rows = jnp.dot(order, dense[i * 256 : i * 256 + 256, :], preferred_element_type=jnp.float32).astype(jnp.bfloat16)
-        sums = jnp.dot(rows[:, :depth], right_ref[...], preferred_element_type=jnp.float32) + jnp.dot(
-            rows[:, depth:], right2_ref[...], preferred_element_type=jnp.float32
-        )
-        parts = sums.shape[1] // LANES
-        for q in range(parts):
-            out_ref[pl.ds(i * size * parts + q, size, stride=parts), :] = sums[:, q * LANES : (q + 1) * LANES]
+        ordered[i * size : i * size + size, :] = jnp.dot(
+            order, dense[i * 256 : i * 256 + 256, :], preferred_element_type=jnp.float32
+        ).astype(jnp.bfloat16)
+    sums = jnp.dot(ordered[:, :depth], right_ref[...], preferred_element_type=jnp.float32) + jnp.dot(
+        ordered[:, depth:], right2_ref[...], preferred_element_type=jnp.float32
+    )
+    parts = sums.shape[1] // LANES
+    for q in range(parts):
+        out_ref[pl.ds(q, 2 * size, stride=parts), :] = sums[:, q * LANES : (q + 1) * LANES]
 
 
 def pack(marks, left):
@@ -151,6 +153,7 @@
         out_specs=[pl.BlockSpec(memory_space=pltpu.VMEM), pl.BlockSpec(memory_space=pltpu.SMEM)],
         scratch_shapes=[
             pltpu.VMEM((512, 2 * depth), jnp.bfloat16),
+            pltpu.VMEM((64 * slots, 2 * depth), jnp.bfloat16),
             pltpu.VMEM((16, LANES), jnp.int32),
             pltpu.SMEM((16, LANES), jnp.int32),
             pltpu.SemaphoreType.DMA,
@@ -184,7 +187,7 @@
     before = jnp.sum(owned[:, None] & (number[:, None] < number[None, :]), axis=0)
     panel_of_slot = jnp.sum(jnp.where(owned[None, :] & (before[None, :] == number[:slots, None]), number[None, :], 0), axis=1)
     chosen = jnp.take(product.reshape(8, 32, 2 * width // LANES, LANES), panel_of_slot, axis=0)
-    return chosen.transpose(1, 0, 2, 3).reshape(-1, LANES)
+    return lax.optimization_barrier(chosen.transpose(1, 0, 2, 3).reshape(-1, LANES))
 
 
 def update(slab, chosen, sums):
@@ -206,12 +209,15 @@
 
     def reduced(slots):
         def branch():
+            def to_wire(product):
+                return (product * WIRE_SCALE).astype(WIRE).reshape(32, slots, TILE, LANES)
+
             product, flag = unpack_product(slots, core, owners, got, right, right2)
-            product = lax.switch(
+            parts = to_wire(product)
+            parts = lax.switch(
                 flag[0],
-                [lambda: product, lambda: dense_product(slots, core, owners, left, right, right2, occupancy)],
+                [lambda: parts, lambda: to_wire(dense_product(slots, core, owners, left, right, right2, occupancy))],
             )
-            parts = (product * WIRE_SCALE).astype(WIRE).reshape(32, slots, TILE, LANES)
             came = lax.all_to_all(parts, ("zhi", "y"), 0, 0, tiled=True)
             sums = jnp.sum(came.astype(jnp.float32), axis=0) * (1.0 / WIRE_SCALE)
             return update(slab, slot_of_step[:, None] == jnp.arange(slots)[None, :], sums)

time: 59.9 us -> 55.4 us (0.925)
  waiting for transfers between devices: 21.3 us -> 18.7 us
  Pallas kernels: 6.42 us -> 5.37 us
  local copies, waits for them, and re-layouts: 1.45 us -> 0.65 us
    all_to_all x1, waiting for transfers between devices: 16.3 us -> 13.7 us  [branch(): came = lax.all_to_all(parts, ('zhi', 'y'), 0, 0, tiled=True)]
    pallas_call x1, Pallas kernels: 4.11 us -> 2.98 us  [unpack_product(): pl.pallas_call(functools.partial(product_kernel, slots), out_shape=[jax.S...]
    cond x2 -> x0, local copies, waits for them, and re-layouts: 0.8 us -> none
where the time goes in v7:
time: 55.4 us; the launch traced here: 55.1 us
  starting transfers between devices  23.9 us (43%)
  waiting for transfers between devices  18.7 us (34%)
  Pallas kernels  5.37 us (10%)
  between operations  3.33 us (6%)
  other arithmetic  1.87 us (3%)
  loops' own time  1.24 us (2%)
  local copies, waits for them, and re-layouts  0.65 us (1%)
    all_to_all x1, starting transfers between devices, branch(): came = lax.all_to_all(parts, ('zhi', 'y'), 0, 0, tiled=True)  15.4 us
    all_to_all x1, waiting for transfers between devices, branch(): came = lax.all_to_all(parts, ('zhi', 'y'), 0, 0, tiled=True)  13.7 us
    all_to_all x1, starting transfers between devices, body(): got = lax.all_to_all(packed, ('core', 'zlo', 'x'), 0, 0, tiled=True)  6.21 us
    all_to_all x1, waiting for transfers between devices, body(): got = lax.all_to_all(packed, ('core', 'zlo', 'x'), 0, 0, tiled=True)  4.98 us
    pallas_call x1, Pallas kernels, unpack_product(): pl.pallas_call(functools.partial(product_kernel, slots), out_shape=[jax.S...  2.98 us
    pallas_call x1, Pallas kernels, pack(): pl.pallas_call(pack_kernel, out_shape=jax.ShapeDtypeStruct((16, PACKED_RO...  2.38 us
    ppermute x1, starting transfers between devices, body(): right2 = lax.ppermute(right, 'core', [(0, 1), (1, 0)])  2.32 us
    another operation x1, loops' own time, body(): return lax.switch(which, [reduced(slots) for slots in DISTINCT])  1.23 us
  transfers between devices with their start and end apart: 3, of which 2 were waited for; matrix products, arithmetic and copies ran while one was open for 2% of the time, Pallas kernels for 0%

profile of v7, /device:TPU:8, one launch (start us, length us, event | category | flops | bytes accessed | tf_op | source)
XLA Modules:
  0.0 55.1 jit_solution(7870295857678257736)
XLA Ops:
  0.0 0.0 copy-start.3
  0.0 0.0 copy-start.1
  0.0 0.0 copy-start.5
  0.0 0.0 copy-start
  0.0 0.0 copy-start.2
  0.0 2.4 %shard_map.67 = bf16[16,144,128]{2,1,0:T(8,128)(2,1)} custom-call(s32[2,12]{1,0:T(2,128)} %marks_ref.1, bf16[128,768]{1,0:T(8,128)(2,1)} %left_ref.1), custom_call_target="tpu_custom_call" | custom-call | tf_op jit(solution)/shard_map/pallas_call | solution.py:132
  2.4 6.2 %all-to-all-start.12 = ((bf16[16,144,128]{2,1,0:T(8,128)(2,1)}), bf16[16,144,128]{2,1,0:T(8,128)(2,1)S(1)}, u32[]{:S(2)}, u32[]{:S(2)}) async-start(bf16[16,144,128]{2,1,0:T(8,128)(2,1)} %shard_map.67), calls=%async_computation.12 | async-start | bytes 1179648 | tf_op jit(solution)/shard_map/all_to_all | solution.py:204
  8.6 0.0 copy-done
  8.6 2.3 %collective-permute-start = (bf16[768,512]{1,0:T(8,128)(2,1)S(1)}, bf16[768,512]{1,0:T(8,128)(2,1)S(1)}, u32[]{:S(2)}, u32[]{:S(2)}) collective-permute-start(bf16[768,512]{1,0:T(8,128)(2,1)S(1)} %copy-done), channel_id=1, source_target_pairs={{0,8},{8,0},{1,9},{9,1},{2,10},{10,2},{3,11},{11,3},{4,12},{12,4},... | collective-permute-start | bytes 2359304 | tf_op jit(solution)/shard_map/ppermute | solution.py:202
  11.0 0.0 copy-done.5
  11.0 0.1 fusion.253
  11.1 0.6 %convert_reduce_fusion.12 = s32[]{:T(128)} fusion(pred[8]{0:T(512)(128)(4,1)S(1)} %fusion.253), kind=kLoop, calls=%fused_computation.463 | loop fusion | flops 15 | bytes 12 | tf_op jit(solution)/shard_map/reduce_sum | solution.py:207
  15.0 0.1 fusion.255
  15.0 0.0 collective-permute-done
  15.0 5.0 %all-to-all-done.12 = bf16[16,144,128]{2,1,0:T(8,128)(2,1)S(1)} async-done(((bf16[16,144,128]{2,1,0:T(8,128)(2,1)}), bf16[16,144,128]{2,1,0:T(8,128)(2,1)S(1)}, u32[]{:S(2)}, u32[]{:S(2)}) %all-to-all-start.12) | async-done | bytes 589856 | tf_op jit(solution)/shard_map/all_to_all | solution.py:204
  20.0 0.0 copy-done.3
  20.0 0.0 copy-done.1
  20.0 0.0 copy-done.2
  20.0 34.4 %conditional.7 = (f32[8,2,512]{2,1,0:T(2,128)S(1)}) conditional(s32[]{:T(128)} %clamp.39, (bf16[8,2,512]{2,1,0:T(2,128)(2,1)S(1)}, s32[8,8]{1,0:T(8,128)S(1)}, s32[]{:T(128)}, s32[8]{0:T(128)S(1)}, bf16[16,144,128]{2,1,0:T(8,128)(2,1)S(1)}, /*index=5*/bf16[768,512]{1,0:T(8,128)(2,1)S(1)}, ...), branch_computations={%region_3.11_spmd, %region_11.19_spmd, %region_19.27_spmd, %region... | conditional | flops 1638609408 | bytes 32567412 | solution.py:228
  20.0 3.0 %branch_0_fun.1 = (f32[768,128]{1,0:T(8,128)S(1)}, s32[1]{0:T(128)}) custom-call(s32[1]{0:T(128)} %bitcast.9.core_ref, s32[8]{0:T(128)S(1)} %get-tuple-element.243.owners_ref, bf16[16,144,128]{2,1,0:T(8,128)(2,1)S(1)} %get-tuple-element.244.got_ref, bf16[768,512]{1,0:T(8,128)(2,1)S(1)} %get-tuple-element.245.right_ref, ...), custom_call_target="tpu_custom_call" | custom-call | flops 805306368 | bytes 4194304 | tf_op jit(solution)/shard_map/cond/branch_0_fun/pallas_call | solution.py:146
  23.0 0.7 %multiply_convert_fusion.1 = f16[768,128]{1,0:T(8,128)(2,1)} fusion(f32[768,128]{1,0:T(8,128)S(1)} %get-tuple-element.248), kind=kLoop, calls=%fused_computation.75 | loop fusion | flops 196608 | bytes 589824 | tf_op jit(solution)/shard_map/cond/branch_0_fun/convert_element_type | solution.py:213
  24.4 15.4 %all-to-all-start.1 = ((f16[32,3,8,128]{3,2,1,0:T(8,128)(2,1)}), f16[32,3,8,128]{3,2,1,0:T(8,128)(2,1)S(1)}, u32[]{:S(2)}, u32[]{:S(2)}) async-start(f16[32,3,8,128]{3,2,1,0:T(8,128)(2,1)} %bitcast.11), calls=%async_computation.1 | async-start | bytes 393216 | tf_op jit(solution)/shard_map/cond/branch_0_fun/all_to_all | solution.py:221
  39.8 0.1 reduce_sum.248
  39.9 0.1 iota_compare_fusion.2
  40.0 13.7 %all-to-all-done.1 = f16[32,3,8,128]{3,2,1,0:T(8,128)(2,1)S(1)} async-done(((f16[32,3,8,128]{3,2,1,0:T(8,128)(2,1)}), f16[32,3,8,128]{3,2,1,0:T(8,128)(2,1)S(1)}, u32[]{:S(2)}, u32[]{:S(2)}) %all-to-all-start.1) | async-done | bytes 196640 | tf_op jit(solution)/shard_map/cond/branch_0_fun/all_to_all | solution.py:221
  53.7 0.1 select_reduce_fusion.1
  54.4 0.0 copy-start.4
  54.5 0.6 %copy-done.4 = f32[8,2,512]{2,1,0:T(2,128)} copy-done((f32[8,2,512]{2,1,0:T(2,128)}, f32[8,2,512]{2,1,0:T(2,128)S(1)}, u32[]{:S(2)}) %copy-start.4) | copy-done | bytes 32792
  (6 shorter events, 0.1 us)
Async XLA Ops:
  0.0 20.0 %copy-start.3 = (s32[2,12]{1,0:T(2,128)S(1)}, s32[2,12]{1,0:T(2,128)}, u32[]{:S(2)}) copy-start(s32[2,12]{1,0:T(2,128)} %marks_ref.1) | copy-start | bytes 292
  0.0 20.0 %copy-start.1 = (bf16[128,768]{1,0:T(8,128)(2,1)S(1)}, bf16[128,768]{1,0:T(8,128)(2,1)}, u32[]{:S(2)}) copy-start(bf16[128,768]{1,0:T(8,128)(2,1)} %left_ref.1) | copy-start | bytes 589828
  0.0 11.0 %copy-start.5 = (s32[8]{0:T(128)S(1)}, s32[8]{0:T(128)}, u32[]{:S(2)}) copy-start(s32[8]{0:T(128)} %param.26) | copy-start | bytes 100
  0.0 8.6 %copy-start = (bf16[768,512]{1,0:T(8,128)(2,1)S(1)}, bf16[768,512]{1,0:T(8,128)(2,1)}, u32[]{:S(2)}) copy-start(bf16[768,512]{1,0:T(8,128)(2,1)} %param.24) | copy-start | bytes 2359300
  0.0 20.0 %copy-start.2 = (bf16[8,2,512]{2,1,0:T(2,128)(2,1)S(1)}, bf16[8,2,512]{2,1,0:T(2,128)(2,1)}, u32[]{:S(2)}) copy-start(bf16[8,2,512]{2,1,0:T(2,128)(2,1)} %param.27) | copy-start | bytes 49156
  2.4 17.6 %all-to-all-start.12 = ((bf16[16,144,128]{2,1,0:T(8,128)(2,1)}), bf16[16,144,128]{2,1,0:T(8,128)(2,1)S(1)}, u32[]{:S(2)}, u32[]{:S(2)}) async-start(bf16[16,144,128]{2,1,0:T(8,128)(2,1)} %shard_map.67), calls=%async_computation.12 | async-start | bytes 1179648 | tf_op jit(solution)/shard_map/all_to_all | solution.py:204
  8.6 6.4 %collective-permute-start = (bf16[768,512]{1,0:T(8,128)(2,1)S(1)}, bf16[768,512]{1,0:T(8,128)(2,1)S(1)}, u32[]{:S(2)}, u32[]{:S(2)}) collective-permute-start(bf16[768,512]{1,0:T(8,128)(2,1)S(1)} %copy-done), channel_id=1, source_target_pairs={{0,8},{8,0},{1,9},{9,1},{2,10},{10,2},{3,11},{11,3},{4,12},{12,4},... | collective-permute-start | bytes 2359304 | tf_op jit(solution)/shard_map/ppermute | solution.py:202
  24.4 29.3 %all-to-all-start.1 = ((f16[32,3,8,128]{3,2,1,0:T(8,128)(2,1)}), f16[32,3,8,128]{3,2,1,0:T(8,128)(2,1)S(1)}, u32[]{:S(2)}, u32[]{:S(2)}) async-start(f16[32,3,8,128]{3,2,1,0:T(8,128)(2,1)} %bitcast.11), calls=%async_computation.1 | async-start | bytes 393216 | tf_op jit(solution)/shard_map/cond/branch_0_fun/all_to_all | solution.py:221
  54.4 0.6 %copy-start.4 = (f32[8,2,512]{2,1,0:T(2,128)}, f32[8,2,512]{2,1,0:T(2,128)S(1)}, u32[]{:S(2)}) copy-start(f32[8,2,512]{2,1,0:T(2,128)S(1)} %get-tuple-element.574) | copy-start | bytes 98308

commit v8 on v7

--- a/solution.py
+++ b/solution.py
@@ -14,6 +14,8 @@
 LANES = 128
 TILE = 8
 DISTINCT = (3, 4, 5, 6, 7, 8)
+LAST = 4
+MEMBERS = [(member - LAST) % 32 for member in range(32)]
 PACKED_ROWS = SLOTS // 2 * 32
 LIST_ROWS = 16
 WIRE = jnp.float16
@@ -62,31 +64,33 @@
         out_ref[to, PACKED_ROWS:, :] = listed.astype(jnp.bfloat16)
 
 
-def destination_order(owners_ref, slots):
+def destination_order(places, row_of_owners, slots):
     place = lax.broadcasted_iota(jnp.int32, (32 * slots, 1), 0)
     at = sum((place >= k * 2 * slots).astype(jnp.int32) for k in range(1, 16))
     slot, b = (place - at * (2 * slots)) // 2, place % 2
     wanted = at * 2 + b
     filled = jnp.int32(0)
+    owners = [places[row_of_owners, t] for t in range(8)]
     for panel in range(8):
-        owned = functools.reduce(jnp.logical_or, [owners_ref[t] == panel for t in range(owners_ref.shape[0])])
+        owned = functools.reduce(jnp.logical_or, [owner == panel for owner in owners])
         wanted = wanted + jnp.where(slot == jnp.where(owned, filled, slots), panel * 32, 0)
         filled = filled + owned.astype(jnp.int32)
     row = lax.broadcasted_iota(jnp.int32, (32 * slots, 256), 1)
     return (row == wanted).astype(jnp.bfloat16)
 
 
-def product_kernel(slots, core_ref, owners_ref, got_ref, right_ref, right2_ref, out_ref, flag_ref, dense, ordered, lists, places, sem):
+def product_kernel(slots, facts_ref, got_ref, right_ref, right2_ref, out_ref, flag_ref, dense, ordered, lists, places, sem):
     sources = got_ref.shape[0]
     depth = right_ref.shape[0]
-    core = core_ref[0]
+    lists[sources : sources + 1, :] = facts_ref[...]
     for source in range(sources):
         lists[source : source + 1, :] = got_ref[source, PACKED_ROWS : PACKED_ROWS + 1, :].astype(jnp.int32)
     copy = pltpu.make_async_copy(lists, places, sem)
     copy.start()
     dense[...] = jnp.zeros_like(dense)
-    order = destination_order(owners_ref, slots)
     copy.wait()
+    core = places[sources, 8]
+    order = destination_order(places, sources, slots)
     side_of_lane = lax.broadcasted_iota(jnp.int32, (32, LANES), 1) // ATOM_BLOCK
 
     def put(source, first, slots_here):
@@ -124,8 +128,11 @@
         ordered[:, depth:], right2_ref[...], preferred_element_type=jnp.float32
     )
     parts = sums.shape[1] // LANES
+    first = LAST * 2 * slots
     for q in range(parts):
-        out_ref[pl.ds(q, 2 * size, stride=parts), :] = sums[:, q * LANES : (q + 1) * LANES]
+        columns = sums[:, q * LANES : (q + 1) * LANES]
+        out_ref[pl.ds(q, first, stride=parts), :] = columns[2 * size - first :]
+        out_ref[pl.ds(first * parts + q, 2 * size - first, stride=parts), :] = columns[: 2 * size - first]
 
 
 def pack(marks, left):
@@ -141,7 +148,7 @@
     )(marks, left)
 
 
-def unpack_product(slots, core, owners, got, right, right2):
+def unpack_product(slots, facts, got, right, right2):
     depth, width = right.shape
     return pl.pallas_call(
         functools.partial(product_kernel, slots),
@@ -149,18 +156,18 @@
             jax.ShapeDtypeStruct((32 * slots * 2 * (width // LANES), LANES), jnp.float32),
             jax.ShapeDtypeStruct((1,), jnp.int32),
         ],
-        in_specs=[pl.BlockSpec(memory_space=pltpu.SMEM)] * 2 + [pl.BlockSpec(memory_space=pltpu.VMEM)] * 3,
+        in_specs=[pl.BlockSpec(memory_space=pltpu.VMEM)] * 4,
         out_specs=[pl.BlockSpec(memory_space=pltpu.VMEM), pl.BlockSpec(memory_space=pltpu.SMEM)],
         scratch_shapes=[
             pltpu.VMEM((512, 2 * depth), jnp.bfloat16),
             pltpu.VMEM((64 * slots, 2 * depth), jnp.bfloat16),
-            pltpu.VMEM((16, LANES), jnp.int32),
-            pltpu.SMEM((16, LANES), jnp.int32),
+            pltpu.VMEM((24, LANES), jnp.int32),
+            pltpu.SMEM((24, LANES), jnp.int32),
             pltpu.SemaphoreType.DMA,
         ],
         compiler_params=pltpu.CompilerParams(vmem_limit_bytes=24 * 2**20),
         cost_estimate=pl.CostEstimate(flops=2 * 512 * 2 * depth * width, bytes_accessed=4 * 2**20, transcendentals=0),
-    )(core.reshape(1), owners, got, right, right2)
+    )(facts, got, right, right2)
 
 
 def spread_marks(marks):
@@ -187,7 +194,7 @@
     before = jnp.sum(owned[:, None] & (number[:, None] < number[None, :]), axis=0)
     panel_of_slot = jnp.sum(jnp.where(owned[None, :] & (before[None, :] == number[:slots, None]), number[None, :], 0), axis=1)
     chosen = jnp.take(product.reshape(8, 32, 2 * width // LANES, LANES), panel_of_slot, axis=0)
-    return lax.optimization_barrier(chosen.transpose(1, 0, 2, 3).reshape(-1, LANES))
+    return lax.optimization_barrier(jnp.roll(chosen.transpose(1, 0, 2, 3), LAST, axis=0).reshape(-1, LANES))
 
 
 def update(slab, chosen, sums):
@@ -206,19 +213,21 @@
     owned = jnp.any(owners[:, None] == panels[None, :], axis=0)
     number = jnp.sum(owned)
     slot_of_step = jnp.sum(owned[None, :] & (panels[None, :] < owners[:, None]), axis=1)
+
+    facts = jnp.pad(jnp.concatenate([owners, core.reshape(1)]), (0, LANES - 9)).reshape(1, LANES)
 
     def reduced(slots):
         def branch():
             def to_wire(product):
                 return (product * WIRE_SCALE).astype(WIRE).reshape(32, slots, TILE, LANES)
 
-            product, flag = unpack_product(slots, core, owners, got, right, right2)
+            product, flag = unpack_product(slots, facts, got, right, right2)
             parts = to_wire(product)
             parts = lax.switch(
                 flag[0],
                 [lambda: parts, lambda: to_wire(dense_product(slots, core, owners, left, right, right2, occupancy))],
             )
-            came = lax.all_to_all(parts, ("zhi", "y"), 0, 0, tiled=True)
+            came = lax.all_to_all(parts, ("zhi", "y"), 0, 0, axis_index_groups=[MEMBERS], tiled=True)
             sums = jnp.sum(came.astype(jnp.float32), axis=0) * (1.0 / WIRE_SCALE)
             return update(slab, slot_of_step[:, None] == jnp.arange(slots)[None, :], sums)
 

time: 55.4 us -> 53.7 us (0.969)
  the two profiles are of different devices: /device:TPU:8 before, /device:TPU:1 now
where the time goes in v8:
time: 53.7 us; the launch traced here: 53.3 us
  starting transfers between devices  26.2 us (49%)
  waiting for transfers between devices  14.7 us (27%)
  Pallas kernels  5.23 us (10%)
  between operations  3.32 us (6%)
  other arithmetic  2.06 us (4%)
  loops' own time  1.18 us (2%)
  local copies, waits for them, and re-layouts  0.65 us (1%)
    all_to_all x1, starting transfers between devices, branch(): lax.all_to_all(parts, ('zhi', 'y'), 0, 0, axis_index_groups=[MEMBERS], ti...  13.7 us
    all_to_all x1, starting transfers between devices, body(): got = lax.all_to_all(packed, ('core', 'zlo', 'x'), 0, 0, tiled=True)  10.3 us
    all_to_all x1, waiting for transfers between devices, branch(): lax.all_to_all(parts, ('zhi', 'y'), 0, 0, axis_index_groups=[MEMBERS], ti...  9.7 us
    all_to_all x1, waiting for transfers between devices, body(): got = lax.all_to_all(packed, ('core', 'zlo', 'x'), 0, 0, tiled=True)  5.03 us
    pallas_call x1, Pallas kernels, unpack_product(): pl.pallas_call(functools.partial(product_kernel, slots), out_shape=[jax.S...  2.72 us
    pallas_call x1, Pallas kernels, pack(): pl.pallas_call(pack_kernel, out_shape=jax.ShapeDtypeStruct((16, PACKED_RO...  2.51 us
    ppermute x1, starting transfers between devices, body(): right2 = lax.ppermute(right, 'core', [(0, 1), (1, 0)])  2.08 us
    another operation x1, loops' own time, body(): return lax.switch(which, [reduced(slots) for slots in DISTINCT])  1.18 us
  transfers between devices with their start and end apart: 3, of which 2 were waited for; matrix products, arithmetic and copies ran while one was open for 2% of the time, Pallas kernels for 0%

profile of v8, /device:TPU:1, one launch (start us, length us, event | category | flops | bytes accessed | tf_op | source)
XLA Modules:
  0.0 53.3 jit_solution(18187596804063111345)
XLA Ops:
  0.0 0.0 copy-start.3
  0.0 0.0 copy-start.1
  0.0 0.0 copy-start.5
  0.0 0.0 copy-start
  0.0 0.0 copy-start.2
  0.0 2.5 %shard_map.67 = bf16[16,144,128]{2,1,0:T(8,128)(2,1)} custom-call(s32[2,12]{1,0:T(2,128)} %marks_ref.1, bf16[128,768]{1,0:T(8,128)(2,1)} %left_ref.1), custom_call_target="tpu_custom_call" | custom-call | tf_op jit(solution)/shard_map/pallas_call | solution.py:139
  2.5 10.3 %all-to-all-start.12 = ((bf16[16,144,128]{2,1,0:T(8,128)(2,1)}), bf16[16,144,128]{2,1,0:T(8,128)(2,1)S(1)}, u32[]{:S(2)}, u32[]{:S(2)}) async-start(bf16[16,144,128]{2,1,0:T(8,128)(2,1)} %shard_map.67), calls=%async_computation.12 | async-start | bytes 1179648 | tf_op jit(solution)/shard_map/all_to_all | solution.py:211
  12.9 0.0 copy-done
  12.9 2.1 %collective-permute-start = (bf16[768,512]{1,0:T(8,128)(2,1)S(1)}, bf16[768,512]{1,0:T(8,128)(2,1)S(1)}, u32[]{:S(2)}, u32[]{:S(2)}) collective-permute-start(bf16[768,512]{1,0:T(8,128)(2,1)S(1)} %copy-done), channel_id=1, source_target_pairs={{0,8},{8,0},{1,9},{9,1},{2,10},{10,2},{3,11},{11,3},{4,12},{12,4},... | collective-permute-start | bytes 2359304 | tf_op jit(solution)/shard_map/ppermute | solution.py:209
  15.0 0.0 copy-done.5
  15.0 0.1 fusion.253
  15.1 0.6 %convert_reduce_fusion.12 = s32[]{:T(128)} fusion(pred[8]{0:T(512)(128)(4,1)S(1)} %fusion.253), kind=kLoop, calls=%fused_computation.476 | loop fusion | flops 15 | bytes 12 | tf_op jit(solution)/shard_map/reduce_sum | solution.py:214
  19.0 0.1 pad_add_fusion
  19.0 0.1 fusion.255
  19.1 0.0 collective-permute-done
  19.1 5.0 %all-to-all-done.12 = bf16[16,144,128]{2,1,0:T(8,128)(2,1)S(1)} async-done(((bf16[16,144,128]{2,1,0:T(8,128)(2,1)}), bf16[16,144,128]{2,1,0:T(8,128)(2,1)S(1)}, u32[]{:S(2)}, u32[]{:S(2)}) %all-to-all-start.12) | async-done | bytes 589856 | tf_op jit(solution)/shard_map/all_to_all | solution.py:211
  24.1 0.0 copy-done.3
  24.2 0.0 copy-done.1
  24.2 0.0 copy-done.2
  24.2 28.6 %conditional.7 = (f32[8,2,512]{2,1,0:T(2,128)S(1)}) conditional(s32[]{:T(128)} %clamp.39, (bf16[8,2,512]{2,1,0:T(2,128)(2,1)S(1)}, s32[8,8]{1,0:T(8,128)S(1)}, s32[9]{0:T(128)S(1)}, bf16[16,144,128]{2,1,0:T(8,128)(2,1)S(1)}, bf16[768,512]{1,0:T(8,128)(2,1)S(1)}, /*index=5*/bf16[768,512]{1,0:T(8,128)(2,1)S(1)}, ...), branch_computations={%region_3.11_spmd, %region_11.19_spmd, %region_19.27_spmd, %region... | conditional | flops 1638871552 | bytes 36762268 | solution.py:237
  24.2 2.7 %branch_2_fun.1 = (f32[1280,128]{1,0:T(8,128)S(1)}, s32[1]{0:T(128)}) custom-call(s32[1,128]{1,0:T(1,128)S(1)} %pad_bitcast_fusion.2.facts_ref, bf16[16,144,128]{2,1,0:T(8,128)(2,1)S(1)} %get-tuple-element.291.got_ref, bf16[768,512]{1,0:T(8,128)(2,1)S(1)} %get-tuple-element.292.right_ref, bf16[768,512]{1,0:T(8,128)(2,1)S(1)} %get-tuple-element.293.right2_ref), custom_call_target="tpu_custom_call" | custom-call | flops 805306368 | bytes 4194304 | tf_op jit(solution)/shard_map/cond/branch_2_fun/pallas_call | solution.py:153
  26.9 0.8 %multiply_convert_fusion.5 = f16[1280,128]{1,0:T(8,128)(2,1)} fusion(f32[1280,128]{1,0:T(8,128)S(1)} %get-tuple-element.295), kind=kLoop, calls=%fused_computation.230 | loop fusion | flops 327680 | bytes 983040 | tf_op jit(solution)/shard_map/cond/branch_2_fun/convert_element_type | solution.py:222
  28.3 13.7 %all-to-all-start.5 = ((f16[32,5,8,128]{3,2,1,0:T(8,128)(2,1)}), f16[32,5,8,128]{3,2,1,0:T(8,128)(2,1)S(1)}, u32[]{:S(2)}, u32[]{:S(2)}) async-start(f16[32,5,8,128]{3,2,1,0:T(8,128)(2,1)} %bitcast.35), calls=%async_computation.5 | async-start | bytes 655360 | tf_op jit(solution)/shard_map/cond/branch_2_fun/all_to_all | solution.py:230
  42.0 0.1 reduce_sum.250
  42.2 0.1 iota_compare_fusion.8
  42.2 9.7 %all-to-all-done.5 = f16[32,5,8,128]{3,2,1,0:T(8,128)(2,1)S(1)} async-done(((f16[32,5,8,128]{3,2,1,0:T(8,128)(2,1)}), f16[32,5,8,128]{3,2,1,0:T(8,128)(2,1)S(1)}, u32[]{:S(2)}, u32[]{:S(2)}) %all-to-all-start.5) | async-done | bytes 327712 | tf_op jit(solution)/shard_map/cond/branch_2_fun/all_to_all | solution.py:230
  51.9 0.1 convert_reduce_fusion.5
  52.0 0.1 select_reduce_fusion.5
  52.7 0.0 copy-start.4
  52.7 0.6 %copy-done.4 = f32[8,2,512]{2,1,0:T(2,128)} copy-done((f32[8,2,512]{2,1,0:T(2,128)}, f32[8,2,512]{2,1,0:T(2,128)S(1)}, u32[]{:S(2)}) %copy-start.4) | copy-done | bytes 32792
  (6 shorter events, 0.1 us)
Async XLA Ops:
  0.0 24.2 %copy-start.3 = (s32[2,12]{1,0:T(2,128)S(1)}, s32[2,12]{1,0:T(2,128)}, u32[]{:S(2)}) copy-start(s32[2,12]{1,0:T(2,128)} %marks_ref.1) | copy-start | bytes 292
  0.0 24.2 %copy-start.1 = (bf16[128,768]{1,0:T(8,128)(2,1)S(1)}, bf16[128,768]{1,0:T(8,128)(2,1)}, u32[]{:S(2)}) copy-start(bf16[128,768]{1,0:T(8,128)(2,1)} %left_ref.1) | copy-start | bytes 589828
  0.0 15.0 %copy-start.5 = (s32[8]{0:T(128)S(1)}, s32[8]{0:T(128)}, u32[]{:S(2)}) copy-start(s32[8]{0:T(128)} %param.26) | copy-start | bytes 100
  0.0 12.9 %copy-start = (bf16[768,512]{1,0:T(8,128)(2,1)S(1)}, bf16[768,512]{1,0:T(8,128)(2,1)}, u32[]{:S(2)}) copy-start(bf16[768,512]{1,0:T(8,128)(2,1)} %param.24) | copy-start | bytes 2359300
  0.0 24.1 %copy-start.2 = (bf16[8,2,512]{2,1,0:T(2,128)(2,1)S(1)}, bf16[8,2,512]{2,1,0:T(2,128)(2,1)}, u32[]{:S(2)}) copy-start(bf16[8,2,512]{2,1,0:T(2,128)(2,1)} %param.27) | copy-start | bytes 49156
  2.5 21.6 %all-to-all-start.12 = ((bf16[16,144,128]{2,1,0:T(8,128)(2,1)}), bf16[16,144,128]{2,1,0:T(8,128)(2,1)S(1)}, u32[]{:S(2)}, u32[]{:S(2)}) async-start(bf16[16,144,128]{2,1,0:T(8,128)(2,1)} %shard_map.67), calls=%async_computation.12 | async-start | bytes 1179648 | tf_op jit(solution)/shard_map/all_to_all | solution.py:211
  12.9 6.2 %collective-permute-start = (bf16[768,512]{1,0:T(8,128)(2,1)S(1)}, bf16[768,512]{1,0:T(8,128)(2,1)S(1)}, u32[]{:S(2)}, u32[]{:S(2)}) collective-permute-start(bf16[768,512]{1,0:T(8,128)(2,1)S(1)} %copy-done), channel_id=1, source_target_pairs={{0,8},{8,0},{1,9},{9,1},{2,10},{10,2},{3,11},{11,3},{4,12},{12,4},... | collective-permute-start | bytes 2359304 | tf_op jit(solution)/shard_map/ppermute | solution.py:209
  28.3 23.6 %all-to-all-start.5 = ((f16[32,5,8,128]{3,2,1,0:T(8,128)(2,1)}), f16[32,5,8,128]{3,2,1,0:T(8,128)(2,1)S(1)}, u32[]{:S(2)}, u32[]{:S(2)}) async-start(f16[32,5,8,128]{3,2,1,0:T(8,128)(2,1)} %bitcast.35), calls=%async_computation.5 | async-start | bytes 655360 | tf_op jit(solution)/shard_map/cond/branch_2_fun/all_to_all | solution.py:230
  52.7 0.6 %copy-start.4 = (f32[8,2,512]{2,1,0:T(2,128)}, f32[8,2,512]{2,1,0:T(2,128)S(1)}, u32[]{:S(2)}) copy-start(f32[8,2,512]{2,1,0:T(2,128)S(1)} %get-tuple-element.634) | copy-start | bytes 98308
